TPU v7x, 768 devices: a whole 4x8x12 slice. The times are simulated.
768 devices in a mesh: row: 8 (over z_hi, core), col: 96 (over x, y, z_lo).
Axes of the slice: x: 4, y: 8, z: 12 (z_hi: 4, z_lo: 3; z = z_hi * 3 + z_lo), core: 2. Of those that a mesh axis runs over, the one named last changes fastest.
Arguments:
- features: bfloat16 [98304, 128], P(('row', 'col')), may hold values from -6 to 6
- adj_blocks: bfloat16 [36864, 128, 128], P(('row', 'col')), as said below
- positions: int32 [768, 48], P(('row', 'col')), may hold values from 0 to 767, as said below
- counts: int32 [768], P(('row', 'col')), may hold values from 1 to 48, as said below
- w_in: bfloat16 [128, 256], replicated, may hold values from -0.5 to 0.5
- w_out: bfloat16 [256, 128], replicated, may hold values from -0.375 to 0.375
- cotangent: bfloat16 [98304, 128], P(('row', 'col')), may hold values from -0.01953125 to 0.01953125
Outputs:
- output: bfloat16 [98304, 128], P(('row', 'col'))
- grad_in: float32 [128, 256], replicated
- grad_out: float32 [256, 128], replicated
Inputs may be any that keep to these rules, and one draw needn't show every extreme that they name: Each device's 48 positions are distinct tile positions; position p names output block p // 96 and input block p % 96. `counts`: the number of live slots of each device, counted from slot 0; later slots hold data that is not part of the adjacency. `adj_blocks`: entries are zero or positive; the share of nonzero entries differs from block to block.
All inputs are finite; a program needn't handle non-finite values.
Results may differ from a plain program's by a relative error of at most 0.003.
The roundings to bfloat16 on the way count: a program that leaves them out, or rounds other values in their place, can miss the bound.
Values may be sent and summed in bfloat16 or wider, within the bound.
No kernel may reach another device: no remote copies, remote signals or barrier semaphores. Data moves between devices by JAX's collectives and lax.ppermute only.
A program may use at most 64 MiB of HBM per device.

v0:
```python
import jax
import jax.numpy as jnp
from jax import lax
from jax.sharding import PartitionSpec as P


def local(features, adj_blocks, positions, counts, w_in, w_out, cotangent):
    block_size = adj_blocks.shape[1]
    slot_count = adj_blocks.shape[0]
    nodes_dev = features.shape[0]
    out_blocks = lax.axis_size("row") * nodes_dev // block_size
    in_blocks = lax.axis_size("col") * nodes_dev // block_size
    places = positions[0]
    live_mask = (jnp.arange(slot_count) < counts[0]).astype(jnp.float32)
    out_index = places // in_blocks
    in_index = places % in_blocks
    out_table = (out_index[:, None] == jnp.arange(out_blocks)[None, :]).astype(
        jnp.float32
    ) * live_mask[:, None]
    in_table = (in_index[:, None] == jnp.arange(in_blocks)[None, :]).astype(
        jnp.float32
    ) * live_mask[:, None]

    def collect(node_rows):
        return lax.all_gather(node_rows, "col", axis=0, tiled=True)

    def aggregate(group_rows):
        width = group_rows.shape[1]
        picked = group_rows.reshape(in_blocks, block_size, width)[in_index]
        products = jnp.einsum(
            "kij,kjf->kif", adj_blocks, picked, preferred_element_type=jnp.float32
        )
        partial_value = jnp.einsum(
            "kr,kif->rif", out_table, products, precision=lax.Precision.HIGHEST
        )
        partial_value = partial_value.reshape(out_blocks * block_size, width)
        return lax.psum_scatter(partial_value, "row", scatter_dimension=0, tiled=True)

    s_one = aggregate(collect(features)).astype(jnp.bfloat16)
    hidden = jnp.maximum(jnp.dot(s_one, w_in, preferred_element_type=jnp.float32), 0.0).astype(
        jnp.bfloat16
    )
    class_rows = collect(
        jnp.dot(hidden, w_out, preferred_element_type=jnp.float32).astype(jnp.bfloat16)
    )
    output = aggregate(class_rows).astype(jnp.bfloat16)
    s_one, hidden, output = (s_one, hidden, output)
    width = cotangent.shape[1]
    group_grad = lax.all_gather(cotangent, "row", axis=0, tiled=True)
    picked = group_grad.reshape(out_blocks, block_size, width)[out_index]
    products = jnp.einsum("kji,kjf->kif", adj_blocks, picked, preferred_element_type=jnp.float32)
    partial_value = jnp.einsum("kc,kif->cif", in_table, products, precision=lax.Precision.HIGHEST)
    partial_value = partial_value.reshape(in_blocks * block_size, width)
    d_two = lax.psum_scatter(partial_value, "col", scatter_dimension=0, tiled=True).astype(
        jnp.bfloat16
    )
    local_out = jnp.einsum("nh,nc->hc", hidden, d_two, preferred_element_type=jnp.float32)
    d_hidden = jnp.einsum("nc,hc->nh", d_two, w_out, preferred_element_type=jnp.float32)
    masked = jnp.where(hidden > 0, d_hidden, 0.0).astype(jnp.bfloat16)
    local_in = jnp.einsum("nf,nh->fh", s_one, masked, preferred_element_type=jnp.float32)
    grad_in, grad_out = lax.psum((local_in, local_out), ("row", "col"))
    return (output, grad_in, grad_out)


def solution(mesh):
    placed = (
        P(("row", "col"), None),
        P(("row", "col"), None, None),
        P(("row", "col"), None),
        P(("row", "col")),
        P(),
        P(),
        P(("row", "col"), None),
    )
    return jax.shard_map(
        local,
        mesh=mesh,
        in_specs=placed,
        out_specs=(P(("row", "col"), None), P(), P()),
        check_vma=False,
    )
```

profile of v0, /device:TPU:1, one launch (start us, length us, event | category | flops | bytes accessed | tf_op | source)
XLA Modules:
  0.0 2270.4 jit_solution(8645773811426781752)
XLA Ops:
  10.5 433.3 %all-gather.3.cloned.1.call-done = bf16[12288,128]{1,0:T(8,128)(2,1)} async-done(((bf16[128,128]{1,0:T(8,128)(2,1)}), bf16[12288,128]{1,0:T(8,128)(2,1)}) %all-gather.3.cloned.1.call-update) | async-done | bytes 3145744 | tf_op jit(solution)/shard_map/all_gather | solution.py:25
  443.7 2.7 gather_fusion
  446.5 2.9 fusion.42
  449.4 3.6 copy.13
  453.0 3.5 fusion.4
  457.5 156.6 %reduce-scatter.4.cloned.1.call-done = f32[128,128]{1,0:T(8,128)} async-done(((f32[1024,128]{1,0:T(8,128)}), f32[128,128]{1,0:T(8,128)}) %reduce-scatter.4.cloned.1.call-update) | async-done | bytes 65552 | tf_op jit(solution)/shard_map/reduce_scatter | solution.py:37
  615.9 20.2 all_gather.11
  637.0 2.3 fusion.44
  639.3 3.6 copy.15
  643.0 7.2 fusion
  650.2 6.3 copy.12
  656.8 385.8 %all-gather.5.cloned.1.call-done = bf16[12288,128]{1,0:T(8,128)(2,1)} async-done(((bf16[128,128]{1,0:T(8,128)(2,1)}), bf16[12288,128]{1,0:T(8,128)(2,1)}) %all-gather.5.cloned.1.call-update) | async-done | bytes 3145744 | tf_op jit(solution)/shard_map/all_gather | solution.py:25
  1042.6 2.7 gather_fusion.1
  1045.4 3.0 fusion.43
  1048.3 3.6 copy.14
  1052.0 3.5 fusion.2
  1056.4 558.5 %reduce-scatter.8.cloned.1.call-done = f32[128,128]{1,0:T(8,128)} async-done(((f32[12288,128]{1,0:T(8,128)}), f32[128,128]{1,0:T(8,128)}) %reduce-scatter.8.cloned.1.call-update) | async-done | bytes 65552 | tf_op jit(solution)/shard_map/reduce_scatter | solution.py:54
  1615.0 1.7 fusion.14
  1616.6 1.8 fusion.8
  1618.5 167.8 %reduce-scatter.6.cloned.1.call-done = f32[128,128]{1,0:T(8,128)} async-done(((f32[1024,128]{1,0:T(8,128)}), f32[128,128]{1,0:T(8,128)}) %reduce-scatter.6.cloned.1.call-update) | async-done | bytes 65552 | tf_op jit(solution)/shard_map/reduce_scatter | solution.py:37
  1786.3 1.5 convert_element_type.31
  1787.7 472.7 %all-reduce.3.cloned.1.call-done = (f32[128,256]{1,0:T(8,128)}, f32[256,128]{1,0:T(8,128)}) async-done(((f32[128,256]{1,0:T(8,128)}, f32[256,128]{1,0:T(8,128)}), (f32[128,256]{1,0:T(8,128)}, f32[256,128]{1,0:T(8,128)})) %all-reduce.3.cloned.1.call-update) | async-done | bytes 262160 | tf_op jit(solution)/shard_map/psum | solution.py:61
  2260.4 1.6 copy.19
  2262.0 1.6 copy.20
  (34 shorter events, 7.5 us)
Async XLA Ops:
  7.2 439.3 %copy-start = (bf16[48,128,128]{2,1,0:T(8,128)(2,1)S(1)}, bf16[48,128,128]{2,1,0:T(8,128)(2,1)}, u32[]{:S(2)}) copy-start(bf16[48,128,128]{2,1,0:T(8,128)(2,1)} %param.8) | copy-start | bytes 4718596
  7.2 436.6 %all-gather.3.cloned.1.call-start = ((), (), s32[]{:S(2)}) async-start(), calls=%async_computation.3 | async-start | bytes 3178496 | tf_op jit(solution)/shard_map/all_gather | solution.py:25
  7.9 606.1 %reduce-scatter.4.cloned.1.call-start = ((), (), s32[]{:S(2)}) async-start(), calls=%async_computation.4 | async-start | bytes 589824 | tf_op jit(solution)/shard_map/reduce_scatter | solution.py:37
  456.5 157.6 %copy-start.3 = (bf16[128,256]{1,0:T(8,128)(2,1)S(1)}, bf16[128,256]{1,0:T(8,128)(2,1)}, u32[]{:S(2)}) copy-start(bf16[128,256]{1,0:T(8,128)(2,1)} %param.11) | copy-start | bytes 196612
  456.5 158.5 %copy-start.2 = (bf16[256,128]{1,0:T(8,128)(2,1)S(1)}, bf16[256,128]{1,0:T(8,128)(2,1)}, u32[]{:S(2)}) copy-start(bf16[256,128]{1,0:T(8,128)(2,1)} %param.12) | copy-start | bytes 196612
  456.5 159.4 %copy-start.4 = (bf16[128,128]{1,0:T(8,128)(2,1)S(1)}, bf16[128,128]{1,0:T(8,128)(2,1)}, u32[]{:S(2)}) copy-start(bf16[128,128]{1,0:T(8,128)(2,1)} %param.13) | copy-start | bytes 98308
  457.4 585.2 %all-gather.5.cloned.1.call-start = ((), (), s32[]{:S(2)}) async-start(), calls=%async_computation.5 | async-start | bytes 3178496 | tf_op jit(solution)/shard_map/all_gather | solution.py:25
  615.8 999.1 %reduce-scatter.8.cloned.1.call-start = ((), (), s32[]{:S(2)}) async-start(), calls=%async_computation.7 | async-start | bytes 6356992 | tf_op jit(solution)/shard_map/reduce_scatter | solution.py:54
  639.3 3.6 copy-start.5
  656.5 1129.7 %reduce-scatter.6.cloned.1.call-start = ((), (), s32[]{:S(2)}) async-start(), calls=%async_computation.6 | async-start | bytes 589824 | tf_op jit(solution)/shard_map/reduce_scatter | solution.py:37
  1055.4 561.2 %copy-start.1 = (f32[128,128]{1,0:T(8,128)S(1)}, f32[128,128]{1,0:T(8,128)}, u32[]{:S(2)}) copy-start(f32[128,128]{1,0:T(8,128)} %reduce-scatter.4.cloned.1.call-done) | copy-start | bytes 196612
  1056.4 1204.0 %all-reduce.3.cloned.1.call-start = ((), (), s32[]{:S(2)}) async-start(), calls=%async_computation.8 | async-start | bytes 524288 | tf_op jit(solution)/shard_map/psum | solution.py:61
Sparse Core Ops, SparseCore 0:
  10.4 433.2 all-gather.2
  457.6 156.4 reduce-scatter.3
  617.3 425.2 all-gather.4
  1045.9 569.0 reduce-scatter.7
  1617.9 168.3 reduce-scatter.5
  1793.4 466.9 all-reduce.2
where the time goes:
time: 2270 us
  waiting for transfers between devices  2180 us (96%)
  local copies, waits for them, and re-layouts  28.5 us (1%)
  matrix products  27.7 us (1%)
    all_gather x2, waiting for transfers between devices, collect(): return lax.all_gather(node_rows, 'col', axis=0, tiled=True)  819 us
    reduce_scatter x1, waiting for transfers between devices, local(): lax.psum_scatter(partial_value, 'col', scatter_dimension=0, tiled=True)  559 us
    psum x1, waiting for transfers between devices, local(): grad_in, grad_out = lax.psum((local_in, local_out), ('row', 'col'))  473 us
    reduce_scatter x2, waiting for transfers between devices, aggregate(): lax.psum_scatter(partial_value, 'row', scatter_dimension=0, tiled=True)  324 us
  transfers between devices with their start and end apart: 6, of which 6 were waited for; matrix products, arithmetic and copies ran while one was open for 2% of the time, Pallas kernels for 0%

commit v1 on v0

v1 whole, which is shorter than its diff:
```python
import jax
import jax.numpy as jnp
from jax import lax
from jax.experimental import pallas as pl
from jax.experimental.pallas import tpu as pltpu
from jax.sharding import Mesh
from jax.sharding import PartitionSpec as P

SPLIT = {"zh": 4, "core": 2, "x": 4, "y": 8, "zl": 3}
ROW = ("zh", "core")
COL = ("x", "y", "zl")
ALL = ROW + COL
VMEM_LIMIT = 40 * 1024 * 1024


def forward_kernel(count_ref, place_ref, blocks_ref, rows_ref, sums_ref):
    in_blocks = rows_ref.shape[0]
    sums_ref[...] = jnp.zeros_like(sums_ref)

    def step(slot, carry):
        place = place_ref[0, slot]
        out_block = place // in_blocks
        in_block = place - out_block * in_blocks
        sums_ref[out_block] += jnp.dot(
            blocks_ref[slot], rows_ref[in_block], preferred_element_type=jnp.float32
        )
        return carry

    lax.fori_loop(0, count_ref[0], step, 0)


def backward_kernel(count_ref, place_ref, blocks_ref, rows_ref, sums_ref):
    in_blocks = sums_ref.shape[0]
    sums_ref[...] = jnp.zeros_like(sums_ref)

    def step(slot, carry):
        place = place_ref[0, slot]
        out_block = place // in_blocks
        in_block = place - out_block * in_blocks
        sums_ref[in_block] += lax.dot_general(
            blocks_ref[slot],
            rows_ref[out_block],
            (((0,), (0,)), ((), ())),
            preferred_element_type=jnp.float32,
        )
        return carry

    lax.fori_loop(0, count_ref[0], step, 0)


def tile_product(kernel, counts, positions, adj_blocks, rows, out_blocks, name):
    slots, size, width = adj_blocks.shape[0], adj_blocks.shape[1], rows.shape[2]
    smem = pl.BlockSpec(memory_space=pltpu.SMEM)
    vmem = pl.BlockSpec(memory_space=pltpu.VMEM)
    return pl.pallas_call(
        kernel,
        out_shape=jax.ShapeDtypeStruct((out_blocks, size, width), jnp.float32),
        in_specs=[smem, smem, vmem, vmem],
        out_specs=vmem,
        compiler_params=pltpu.CompilerParams(vmem_limit_bytes=VMEM_LIMIT),
        cost_estimate=pl.CostEstimate(
            flops=2 * slots * size * size * width,
            bytes_accessed=adj_blocks.nbytes + rows.nbytes + 4 * out_blocks * size * width,
            transcendentals=0,
        ),
        name=name,
    )(counts, positions, adj_blocks, rows)


def exchange(values, axes):
    return lax.all_to_all(values, axes, 0, 0)


def collect(node_rows):
    part = lax.all_gather(node_rows, "zl", axis=0)
    part = lax.all_gather(part, "y", axis=0)
    copies = jnp.broadcast_to(part[None], (lax.axis_size("x"),) + part.shape)
    whole = exchange(lax.optimization_barrier(copies), "x")
    return whole.reshape((-1,) + node_rows.shape)


def reduce_rows(partial_value):
    return jnp.sum(exchange(partial_value, ROW), axis=0)


def reduce_cols(partial_value):
    total = partial_value
    for axis in COL:
        size = lax.axis_size(axis)
        total = total.reshape((size, total.shape[0] // size) + total.shape[1:])
        total = jnp.sum(exchange(total, axis), axis=0)
    return total[0]


def sum_everywhere(values):
    width = values.shape[1]
    total = values.reshape(2, -1, width)
    total = jnp.sum(exchange(total, "core"), axis=0)
    planes = lax.axis_size("x") * lax.axis_size("y")
    total = total.reshape(planes, -1, width)
    total = jnp.sum(exchange(total, ("x", "y")), axis=0)
    total = jnp.sum(lax.all_gather(total, ("zh", "zl"), axis=0), axis=0)
    copies = jnp.broadcast_to(total[None], (planes,) + total.shape)
    total = exchange(lax.optimization_barrier(copies), ("x", "y")).reshape(-1, width)
    return lax.all_gather(total, "core", axis=0, tiled=True)


def local(features, adj_blocks, positions, counts, w_in, w_out, cotangent):
    block_size = adj_blocks.shape[1]
    nodes_dev = features.shape[0]
    out_blocks = lax.axis_size(ROW) * nodes_dev // block_size
    in_blocks = lax.axis_size(COL) * nodes_dev // block_size

    def forward(rows, name):
        return tile_product(
            forward_kernel, counts, positions, adj_blocks, rows, out_blocks, name
        )

    group_grad = lax.all_gather(cotangent, ROW, axis=0)
    partial_two = tile_product(
        backward_kernel, counts, positions, adj_blocks, group_grad, in_blocks, "backward"
    )
    d_two = reduce_cols(partial_two).astype(jnp.bfloat16)

    s_one = reduce_rows(forward(collect(features), "forward_one")).astype(jnp.bfloat16)
    hidden = jnp.maximum(jnp.dot(s_one, w_in, preferred_element_type=jnp.float32), 0.0).astype(
        jnp.bfloat16
    )
    class_rows = jnp.dot(hidden, w_out, preferred_element_type=jnp.float32).astype(jnp.bfloat16)
    output = reduce_rows(forward(collect(class_rows), "forward_two")).astype(jnp.bfloat16)

    local_out = jnp.einsum("nh,nc->hc", hidden, d_two, preferred_element_type=jnp.float32)
    d_hidden = jnp.einsum("nc,hc->nh", d_two, w_out, preferred_element_type=jnp.float32)
    masked = jnp.where(hidden > 0, d_hidden, 0.0).astype(jnp.bfloat16)
    local_in = jnp.einsum("nf,nh->fh", s_one, masked, preferred_element_type=jnp.float32)
    width = local_out.shape[1]
    halves = local_in.shape[1] // width
    parts = [local_in[:, i * width : (i + 1) * width] for i in range(halves)]
    grads = sum_everywhere(jnp.concatenate(parts + [local_out], axis=0))
    rows_in = local_in.shape[0]
    grad_in = jnp.concatenate(
        [grads[i * rows_in : (i + 1) * rows_in] for i in range(halves)], axis=1
    )
    grad_out = grads[halves * rows_in :]
    return (output, grad_in, grad_out)


def build(mesh, split):
    cut = Mesh(mesh.devices.reshape(tuple(split.values())), tuple(split))
    placed = (
        P(ALL, None),
        P(ALL, None, None),
        P(ALL, None),
        P(ALL),
        P(),
        P(),
        P(ALL, None),
    )
    return jax.shard_map(
        local,
        mesh=cut,
        in_specs=placed,
        out_specs=(P(ALL, None), P(), P()),
        check_vma=False,
    )


def solution(mesh):
    return build(mesh, SPLIT)
```

time: 2270 us -> 405 us (0.18)
  waiting for transfers between devices: 2180 us -> 160 us
  blocking collectives: 20.2 us -> 147 us
  starting transfers between devices: 0.46 us -> 57.1 us
  matrix products: 27.7 us -> 0.79 us
    reduce_scatter x3 -> x0, waiting for transfers between devices: 883 us -> none  [the longest x1 559 us: local(): lax.psum_scatter(partial_value, 'col', scatter_dimension=0, tiled=True)]
    all_gather x2 -> x0, waiting for transfers between devices: 819 us -> none  [collect(): return lax.all_gather(node_rows, 'col', axis=0, tiled=True)]
    psum x1 -> x0, waiting for transfers between devices: 473 us -> none  [local(): grad_in, grad_out = lax.psum((local_in, local_out), ('row', 'col'))]
    all_to_all x0 -> x9, waiting for transfers between devices: none -> 160 us  [exchange(): return lax.all_to_all(values, axes, 0, 0)]
    all_gather x1 -> x7, blocking collectives: 20.2 us -> 136 us  [the longest x2 43.2 us: collect(): part = lax.all_gather(part, 'y', axis=0)]
    all_to_all x0 -> x9, starting transfers between devices: none -> 57.1 us  [exchange(): return lax.all_to_all(values, axes, 0, 0)]
  transfers between devices with their start and end apart: 6 -> 9, of which waited for: 6 -> 6; matrix products, arithmetic and copies ran while one was open for 2% -> 3% of each run, Pallas kernels for 0% -> 5%
where the time goes in v1:
time: 405 us; the launch traced here: 404 us
  waiting for transfers between devices  160 us (40%)
  blocking collectives  147 us (36%)
  starting transfers between devices  57.1 us (14%)
  Pallas kernels  19.1 us (5%)
  local copies, waits for them, and re-layouts  9.68 us (2%)
  other arithmetic  8.55 us (2%)
    all_to_all x9, waiting for transfers between devices, exchange(): return lax.all_to_all(values, axes, 0, 0)  160 us
    all_to_all x9, starting transfers between devices, exchange(): return lax.all_to_all(values, axes, 0, 0)  57.1 us
    all_gather x2, blocking collectives, collect(): part = lax.all_gather(part, 'y', axis=0)  43.2 us
    all_gather x1, blocking collectives, local(): group_grad = lax.all_gather(cotangent, ROW, axis=0)  33.3 us
    all_gather x1, blocking collectives, sum_everywhere(): total = jnp.sum(lax.all_gather(total, ('zh', 'zl'), axis=0), axis=0)  32.1 us
    pallas_call x3, Pallas kernels, tile_product(): pl.pallas_call(kernel, out_shape=jax.ShapeDtypeStruct((out_blocks, size,...  19.1 us
    all_gather x2, blocking collectives, collect(): part = lax.all_gather(node_rows, 'zl', axis=0)  18.5 us
    all_to_all x1, blocking collectives, exchange(): return lax.all_to_all(values, axes, 0, 0)  11 us
  transfers between devices with their start and end apart: 9, of which 6 were waited for; matrix products, arithmetic and copies ran while one was open for 3% of the time, Pallas kernels for 5%

profile of v1, /device:TPU:1, one launch (start us, length us, event | category | flops | bytes accessed | tf_op | source)
XLA Modules:
  0.0 403.6 jit_solution(10851574659504206351)
XLA Ops:
  0.6 10.4 %all-gather = bf16[384,128]{1,0:T(8,128)(2,1)S(1)} all-gather(bf16[128,128]{1,0:T(8,128)(2,1)} %param.7), channel_id=2, replica_groups=mesh['zh'=4,'core'=2,'x'=4,'y'=8,'zl'=3] {'zl'}, dimensions={0}, use_global_device_ids=true | all-gather | bytes 131072 | tf_op jit(solution)/shard_map/all_gather | solution.py:75
  11.0 22.4 %all-gather.1 = bf16[24,128,128]{2,1,0:T(8,128)(2,1)S(1)} all-gather(bf16[3,128,128]{2,1,0:T(8,128)(2,1)S(1)} %bitcast.34), channel_id=3, replica_groups=mesh['zh'=4,'core'=2,'x'=4,'y'=8,'zl'=3] {'y'}, dimensions={0}, use_global_device_ids=true | all-gather | bytes 884736 | tf_op jit(solution)/shard_map/all_gather | solution.py:76
  35.9 4.8 %all-to-all-start = ((bf16[4,8,3,128,128]{4,3,2,1,0:T(8,128)(2,1)}), bf16[4,8,3,128,128]{4,3,2,1,0:T(8,128)(2,1)}, u32[]{:S(2)}, u32[]{:S(2)}) async-start(bf16[4,8,3,128,128]{4,3,2,1,0:T(8,128)(2,1)} %broadcast_in_dim.7), calls=%async_computation | async-start | bytes 6291456 | tf_op jit(solution)/shard_map/all_to_all | solution.py:71
  41.3 33.3 %all-gather.4 = bf16[1024,128]{1,0:T(8,128)(2,1)S(1)} all-gather(bf16[128,128]{1,0:T(8,128)(2,1)S(1)} %copy-done.6), channel_id=6, replica_groups=mesh['zh'=4,'core'=2,'x'=4,'y'=8,'zl'=3] {'zh','core'}, dimensions={0}, use_global_device_ids=true | all-gather | bytes 294912 | tf_op jit(solution)/shard_map/all_gather | solution.py:119
  74.7 5.9 %backward.1 = f32[96,128,128]{2,1,0:T(8,128)S(1)} custom-call(s32[1]{0:T(128)S(6)} %copy.11.count_ref, s32[1,48]{1,0:T(1,128)S(1)} %copy-done.3, bf16[48,128,128]{2,1,0:T(8,128)(2,1)S(1)} %copy-done.2, bf16[8,128,128]{2,1,0:T(8,128)(2,1)S(1)} %bitcast.27), custom_call_target="tpu_custom_call" | custom-call | flops 201326592 | bytes 8126464 | tf_op jit(solution)/shard_map/backward/pallas_call | solution.py:55
  83.3 5.3 %all-to-all-start.4 = ((f32[4,24,128,128]{3,2,1,0:T(8,128)}), f32[4,24,128,128]{3,2,1,0:T(8,128)}, u32[]{:S(2)}, u32[]{:S(2)}) async-start(f32[4,24,128,128]{3,2,1,0:T(8,128)} %bitcast.26), calls=%async_computation.4 | async-start | bytes 12582912 | tf_op jit(solution)/shard_map/all_to_all | solution.py:71
  88.5 6.6 %forward_one.1 = f32[8,128,128]{2,1,0:T(8,128)} custom-call(s32[1]{0:T(128)S(6)} %copy.11.count_ref, s32[1,48]{1,0:T(1,128)S(1)} %copy-done.3, bf16[48,128,128]{2,1,0:T(8,128)(2,1)S(1)} %copy-done.2, bf16[96,128,128]{2,1,0:T(8,128)(2,1)} %bitcast.2.rows_ref), custom_call_target="tpu_custom_call" | custom-call | flops 201326592 | bytes 5242880 | tf_op jit(solution)/shard_map/forward_one/pallas_call | solution.py:55
  95.1 62.7 %all-to-all-done.4 = f32[4,24,128,128]{3,2,1,0:T(8,128)} async-done(((f32[4,24,128,128]{3,2,1,0:T(8,128)}), f32[4,24,128,128]{3,2,1,0:T(8,128)}, u32[]{:S(2)}, u32[]{:S(2)}) %all-to-all-start.4) | async-done | bytes 6291488 | tf_op jit(solution)/shard_map/all_to_all | solution.py:71
  157.8 7.0 %all-to-all-start.1 = ((f32[8,128,128]{2,1,0:T(8,128)}), f32[8,128,128]{2,1,0:T(8,128)S(1)}, u32[]{:S(2)}, u32[]{:S(2)}) async-start(f32[8,128,128]{2,1,0:T(8,128)} %forward_one.1), calls=%async_computation.1 | async-start | bytes 1048576 | tf_op jit(solution)/shard_map/all_to_all | solution.py:71
  164.9 4.7 %reduce_sum.74 = f32[24,128,128]{2,1,0:T(8,128)} reduce(f32[4,24,128,128]{3,2,1,0:T(8,128)} %all-to-all-done.4, f32[]{:T(128)} %constant.2.clone.1), dimensions={0}, to_apply=%region_2.0 | reduce | flops 1179648 | bytes 7864324 | tf_op jit(solution)/shard_map/reduce_sum | solution.py:91
  169.5 10.4 %all-to-all-done.1 = f32[8,128,128]{2,1,0:T(8,128)S(1)} async-done(((f32[8,128,128]{2,1,0:T(8,128)}), f32[8,128,128]{2,1,0:T(8,128)S(1)}, u32[]{:S(2)}, u32[]{:S(2)}) %all-to-all-start.1) | async-done | bytes 524320 | tf_op jit(solution)/shard_map/all_to_all | solution.py:71
  180.7 12.9 %all-to-all-start.5 = ((f32[8,3,128,128]{3,2,1,0:T(8,128)}), f32[8,3,128,128]{3,2,1,0:T(8,128)S(1)}, u32[]{:S(2)}, u32[]{:S(2)}) async-start(f32[8,3,128,128]{3,2,1,0:T(8,128)} %bitcast.28), calls=%async_computation.5 | async-start | bytes 3145728 | tf_op jit(solution)/shard_map/all_to_all | solution.py:71
  194.8 39.2 %all-to-all-done.5 = f32[8,3,128,128]{3,2,1,0:T(8,128)S(1)} async-done(((f32[8,3,128,128]{3,2,1,0:T(8,128)}), f32[8,3,128,128]{3,2,1,0:T(8,128)S(1)}, u32[]{:S(2)}, u32[]{:S(2)}) %all-to-all-start.5) | async-done | bytes 1572896 | tf_op jit(solution)/shard_map/all_to_all | solution.py:71
  238.3 8.2 %all-gather.2 = bf16[384,128]{1,0:T(8,128)(2,1)S(1)} all-gather(bf16[128,128]{1,0:T(8,128)(2,1)S(1)} %convolution_convert_fusion), channel_id=4, replica_groups=mesh['zh'=4,'core'=2,'x'=4,'y'=8,'zl'=3] {'zl'}, dimensions={0}, use_global_device_ids=true | all-gather | bytes 131072 | tf_op jit(solution)/shard_map/all_gather | solution.py:75
  246.5 20.8 %all-gather.3 = bf16[24,128,128]{2,1,0:T(8,128)(2,1)S(1)} all-gather(bf16[3,128,128]{2,1,0:T(8,128)(2,1)S(1)} %bitcast.33), channel_id=5, replica_groups=mesh['zh'=4,'core'=2,'x'=4,'y'=8,'zl'=3] {'y'}, dimensions={0}, use_global_device_ids=true | all-gather | bytes 884736 | tf_op jit(solution)/shard_map/all_gather | solution.py:76
  270.3 11.0 %all_to_all.50 = f32[2,256,128]{2,1,0:T(8,128)S(1)} all-to-all(f32[2,256,128]{2,1,0:T(8,128)S(1)} %bitcast.31), channel_id=1, replica_groups=mesh['zh'=4,'core'=2,'x'=4,'y'=8,'zl'=3] {'core'}, dimensions={0} | all-to-all | bytes 524288 | tf_op jit(solution)/shard_map/all_to_all | solution.py:71
  281.3 5.9 %all-to-all-start.2 = ((bf16[4,8,3,128,128]{4,3,2,1,0:T(8,128)(2,1)}), bf16[4,8,3,128,128]{4,3,2,1,0:T(8,128)(2,1)}, u32[]{:S(2)}, u32[]{:S(2)}) async-start(bf16[4,8,3,128,128]{4,3,2,1,0:T(8,128)(2,1)} %broadcast_in_dim.8), calls=%async_computation.2 | async-start | bytes 6291456 | tf_op jit(solution)/shard_map/all_to_all | solution.py:71
  287.9 36.5 %all-to-all-done.2 = bf16[4,8,3,128,128]{4,3,2,1,0:T(8,128)(2,1)} async-done(((bf16[4,8,3,128,128]{4,3,2,1,0:T(8,128)(2,1)}), bf16[4,8,3,128,128]{4,3,2,1,0:T(8,128)(2,1)}, u32[]{:S(2)}, u32[]{:S(2)}) %all-to-all-start.2) | async-done | bytes 3145760 | tf_op jit(solution)/shard_map/all_to_all | solution.py:71
  328.5 6.6 %forward_two.1 = f32[8,128,128]{2,1,0:T(8,128)} custom-call(s32[1]{0:T(128)S(6)} %copy.11.count_ref, s32[1,48]{1,0:T(1,128)S(1)} %copy-done.3, bf16[48,128,128]{2,1,0:T(8,128)(2,1)S(1)} %copy-done.2, bf16[96,128,128]{2,1,0:T(8,128)(2,1)} %bitcast.5.rows_ref), custom_call_target="tpu_custom_call" | custom-call | flops 201326592 | bytes 5242880 | tf_op jit(solution)/shard_map/forward_two/pallas_call | solution.py:55
  337.7 9.5 %all-to-all-start.3 = ((f32[8,128,128]{2,1,0:T(8,128)}), f32[8,128,128]{2,1,0:T(8,128)S(1)}, u32[]{:S(2)}, u32[]{:S(2)}) async-start(f32[8,128,128]{2,1,0:T(8,128)} %forward_two.1), calls=%async_computation.3 | async-start | bytes 1048576 | tf_op jit(solution)/shard_map/all_to_all | solution.py:71
  347.2 32.1 %all-gather.5 = f32[96,128]{1,0:T(8,128)S(1)} all-gather(f32[8,128]{1,0:T(8,128)S(1)} %reduce_sum.78), channel_id=7, replica_groups=mesh['zh'=4,'core'=2,'x'=4,'y'=8,'zl'=3] {'zh','zl'}, dimensions={0}, use_global_device_ids=true | all-gather | bytes 53248 | tf_op jit(solution)/shard_map/all_gather | solution.py:102
  379.9 4.2 %all-to-all-start.9 = ((f32[32,8,128]{2,1,0:T(8,128)}), f32[32,8,128]{2,1,0:T(8,128)S(1)}, u32[]{:S(2)}, u32[]{:S(2)}) async-start(f32[32,8,128]{2,1,0:T(8,128)} %broadcast_in_dim.10), calls=%async_computation.9 | async-start | bytes 262144 | tf_op jit(solution)/shard_map/all_to_all | solution.py:71
  384.8 8.5 %all-to-all-done.9 = f32[32,8,128]{2,1,0:T(8,128)S(1)} async-done(((f32[32,8,128]{2,1,0:T(8,128)}), f32[32,8,128]{2,1,0:T(8,128)S(1)}, u32[]{:S(2)}, u32[]{:S(2)}) %all-to-all-start.9) | async-done | bytes 131104 | tf_op jit(solution)/shard_map/all_to_all | solution.py:71
  393.3 8.9 %all_gather.51 = f32[512,128]{1,0:T(8,128)S(1)} all-gather(f32[256,128]{1,0:T(8,128)S(1)} %bitcast.32), channel_id=1, replica_groups=mesh['zh'=4,'core'=2,'x'=4,'y'=8,'zl'=3] {'core'}, dimensions={0}, use_global_device_ids=true | all-gather | bytes 393216 | tf_op jit(solution)/shard_map/all_gather | solution.py:105
  (39 shorter events, 24.5 us)
Async XLA Ops:
  0.6 237.6 %copy-start = (bf16[256,128]{1,0:T(8,128)(2,1)S(1)}, bf16[256,128]{1,0:T(8,128)(2,1)}, u32[]{:S(2)}) copy-start(bf16[256,128]{1,0:T(8,128)(2,1)} %param.12) | copy-start | bytes 196612
  35.9 5.5 %copy-start.6 = (bf16[128,128]{1,0:T(8,128)(2,1)S(1)}, bf16[128,128]{1,0:T(8,128)(2,1)}, u32[]{:S(2)}) copy-start(bf16[128,128]{1,0:T(8,128)(2,1)} %param.13) | copy-start | bytes 98308
  35.9 38.8 %copy-start.2 = (bf16[48,128,128]{2,1,0:T(8,128)(2,1)S(1)}, bf16[48,128,128]{2,1,0:T(8,128)(2,1)}, u32[]{:S(2)}) copy-start(bf16[48,128,128]{2,1,0:T(8,128)(2,1)} %blocks_ref.5) | copy-start | bytes 4718596
  35.9 38.8 %copy-start.3 = (s32[1,48]{1,0:T(1,128)S(1)}, s32[1,48]{1,0:T(1,128)}, u32[]{:S(2)}) copy-start(s32[1,48]{1,0:T(1,128)} %place_ref.5) | copy-start | bytes 580
  35.9 47.4 %all-to-all-start = ((bf16[4,8,3,128,128]{4,3,2,1,0:T(8,128)(2,1)}), bf16[4,8,3,128,128]{4,3,2,1,0:T(8,128)(2,1)}, u32[]{:S(2)}, u32[]{:S(2)}) async-start(bf16[4,8,3,128,128]{4,3,2,1,0:T(8,128)(2,1)} %broadcast_in_dim.7), calls=%async_computation | async-start | bytes 6291456 | tf_op jit(solution)/shard_map/all_to_all | solution.py:71
  80.6 2.7 copy-start.1
  83.3 74.5 %all-to-all-start.4 = ((f32[4,24,128,128]{3,2,1,0:T(8,128)}), f32[4,24,128,128]{3,2,1,0:T(8,128)}, u32[]{:S(2)}, u32[]{:S(2)}) async-start(f32[4,24,128,128]{3,2,1,0:T(8,128)} %bitcast.26), calls=%async_computation.4 | async-start | bytes 12582912 | tf_op jit(solution)/shard_map/all_to_all | solution.py:71
  157.8 22.1 %all-to-all-start.1 = ((f32[8,128,128]{2,1,0:T(8,128)}), f32[8,128,128]{2,1,0:T(8,128)S(1)}, u32[]{:S(2)}, u32[]{:S(2)}) async-start(f32[8,128,128]{2,1,0:T(8,128)} %forward_one.1), calls=%async_computation.1 | async-start | bytes 1048576 | tf_op jit(solution)/shard_map/all_to_all | solution.py:71
  169.5 25.1 %copy-start.5 = (bf16[128,256]{1,0:T(8,128)(2,1)S(1)}, bf16[128,256]{1,0:T(8,128)(2,1)}, u32[]{:S(2)}) copy-start(bf16[128,256]{1,0:T(8,128)(2,1)} %param.11) | copy-start | bytes 196612
  179.9 0.8 copy-start.4
  180.7 53.3 %all-to-all-start.5 = ((f32[8,3,128,128]{3,2,1,0:T(8,128)}), f32[8,3,128,128]{3,2,1,0:T(8,128)S(1)}, u32[]{:S(2)}, u32[]{:S(2)}) async-start(f32[8,3,128,128]{3,2,1,0:T(8,128)} %bitcast.28), calls=%async_computation.5 | async-start | bytes 3145728 | tf_op jit(solution)/shard_map/all_to_all | solution.py:71
  234.8 34.9 %all-to-all-start.6 = ((f32[3,1,128,128]{3,2,1,0:T(8,128)}), f32[3,1,128,128]{3,2,1,0:T(8,128)S(1)}, u32[]{:S(2)}, u32[]{:S(2)}) async-start(f32[3,1,128,128]{3,2,1,0:T(8,128)} %bitcast.10), calls=%async_computation.6 | async-start | bytes 393216 | tf_op jit(solution)/shard_map/all_to_all | solution.py:71
  281.3 43.1 %all-to-all-start.2 = ((bf16[4,8,3,128,128]{4,3,2,1,0:T(8,128)(2,1)}), bf16[4,8,3,128,128]{4,3,2,1,0:T(8,128)(2,1)}, u32[]{:S(2)}, u32[]{:S(2)}) async-start(bf16[4,8,3,128,128]{4,3,2,1,0:T(8,128)(2,1)} %broadcast_in_dim.8), calls=%async_computation.2 | async-start | bytes 6291456 | tf_op jit(solution)/shard_map/all_to_all | solution.py:71
  324.4 13.3 %all-to-all-start.8 = ((f32[32,8,128]{2,1,0:T(8,128)}), f32[32,8,128]{2,1,0:T(8,128)S(1)}, u32[]{:S(2)}, u32[]{:S(2)}) async-start(f32[32,8,128]{2,1,0:T(8,128)} %bitcast.12), calls=%async_computation.8 | async-start | bytes 262144 | tf_op jit(solution)/shard_map/all_to_all | solution.py:71
  337.7 42.3 %all-to-all-start.3 = ((f32[8,128,128]{2,1,0:T(8,128)}), f32[8,128,128]{2,1,0:T(8,128)S(1)}, u32[]{:S(2)}, u32[]{:S(2)}) async-start(f32[8,128,128]{2,1,0:T(8,128)} %forward_two.1), calls=%async_computation.3 | async-start | bytes 1048576 | tf_op jit(solution)/shard_map/all_to_all | solution.py:71
  379.9 13.4 %all-to-all-start.9 = ((f32[32,8,128]{2,1,0:T(8,128)}), f32[32,8,128]{2,1,0:T(8,128)S(1)}, u32[]{:S(2)}, u32[]{:S(2)}) async-start(f32[32,8,128]{2,1,0:T(8,128)} %broadcast_in_dim.10), calls=%async_computation.9 | async-start | bytes 262144 | tf_op jit(solution)/shard_map/all_to_all | solution.py:71

commit v2 on v1

v2 whole, which is shorter than its diff:
```python
import functools

import jax
import jax.numpy as jnp
from jax import lax
from jax.experimental import pallas as pl
from jax.experimental.pallas import tpu as pltpu
from jax.sharding import Mesh
from jax.sharding import PartitionSpec as P

SPLIT = {"zh": 4, "core": 2, "x": 4, "y": 8, "zl": 3}
ROW = ("zh", "core")
COL = ("x", "y", "zl")
ALL = ROW + COL
VMEM_LIMIT = 40 * 1024 * 1024


def ahead_of(place, here, size):
    return lax.rem(place - here + size, size)


def forward_kernel(spans, count_ref, place_ref, here_ref, blocks_ref, *refs):
    rows_refs, sums_ref = refs[:-1], refs[-1]
    per_group = rows_refs[0].shape[0]
    in_blocks = per_group * len(rows_refs)
    sums_ref[...] = jnp.zeros_like(sums_ref)

    def step(slot, carry):
        place = place_ref[0, slot]
        out_block = place // in_blocks
        in_block = place - out_block * in_blocks
        plane = in_block // per_group
        at = in_block - plane * per_group
        back_x = ahead_of(here_ref[0], plane, spans[0])
        for distance, rows_ref in enumerate(rows_refs):

            @pl.when(back_x == distance)
            def add(rows_ref=rows_ref):
                sums_ref[out_block] += jnp.dot(
                    blocks_ref[slot], rows_ref[at], preferred_element_type=jnp.float32
                )

        return carry

    lax.fori_loop(0, count_ref[0], step, 0)


def backward_kernel(spans, count_ref, place_ref, here_ref, blocks_ref, rows_ref, *refs):
    sums_refs, top_ref = refs[:-1], refs[-1]
    in_blocks = spans[0] * spans[1] * spans[2]
    for sums_ref in sums_refs:
        sums_ref[...] = jnp.zeros_like(sums_ref)

    def step(slot, top):
        place = place_ref[0, slot]
        out_block = place // in_blocks
        in_block = place - out_block * in_blocks
        line = in_block // spans[2]
        plane = line // spans[1]
        ahead_x = ahead_of(plane, here_ref[0], spans[0])
        at = in_block - plane * spans[1] * spans[2]
        block = blocks_ref[slot]
        product = lax.dot_general(
            block,
            rows_ref[out_block],
            (((0,), (0,)), ((), ())),
            preferred_element_type=jnp.float32,
        )
        for distance, sums_ref in enumerate(sums_refs):

            @pl.when(ahead_x == distance)
            def add(sums_ref=sums_ref):
                sums_ref[at] += product

        wide = block.astype(jnp.float32).reshape(-1, top.shape[0], top.shape[1])
        return jnp.maximum(top, jnp.max(wide, axis=0))

    top_ref[...] = lax.fori_loop(
        0, count_ref[0], step, jnp.zeros(top_ref.shape, jnp.float32)
    )


def after_kernel(values_ref, earlier_ref, out_ref):
    out_ref[...] = values_ref[...]


def after(values, earlier):
    return pl.pallas_call(
        after_kernel,
        out_shape=jax.ShapeDtypeStruct(values.shape, values.dtype),
        in_specs=[pl.BlockSpec(memory_space=pltpu.VMEM), pl.BlockSpec(memory_space=pl.ANY)],
        out_specs=pl.BlockSpec(memory_space=pltpu.VMEM),
        cost_estimate=pl.CostEstimate(flops=1, bytes_accessed=1, transcendentals=0),
        name="after",
    )(values, earlier)


def tile_product(kernel, counts, positions, here, adj_blocks, rows, outs, name, earlier=()):
    smem = pl.BlockSpec(memory_space=pltpu.SMEM)
    vmem = pl.BlockSpec(memory_space=pltpu.VMEM)
    outs = [jax.ShapeDtypeStruct(shape, jnp.float32) for shape in outs]
    waits = list(earlier)

    def body(count_ref, place_ref, here_ref, *refs):
        kernel(count_ref, place_ref, here_ref, *refs[len(waits) :])

    return pl.pallas_call(
        body,
        out_shape=outs,
        in_specs=[smem] * 3
        + [pl.BlockSpec(memory_space=pl.ANY)] * len(waits)
        + [vmem] * (1 + len(rows)),
        out_specs=[vmem] * len(outs),
        compiler_params=pltpu.CompilerParams(vmem_limit_bytes=VMEM_LIMIT),
        cost_estimate=pl.CostEstimate(flops=1, bytes_accessed=1, transcendentals=0),
        name=name,
    )(counts, positions, here, *waits, adj_blocks, *rows)


def exchange(values, axes):
    return lax.all_to_all(values, axes, 0, 0)


def send_ahead(values, axes, distance):
    size = lax.axis_size(axes)
    return lax.ppermute(values, axes, [(i, (i + distance) % size) for i in range(size)])


def share(values, axes):
    copies = jnp.broadcast_to(values[None], (lax.axis_size(axes),) + values.shape)
    return exchange(lax.optimization_barrier(copies), axes)


def share_x(rows):
    return [rows] + [send_ahead(rows, "x", d) for d in range(1, lax.axis_size("x"))]


def pack(values, power):
    rows = values.shape[-2]
    padded = jnp.pad(values, [(0, 0)] * (values.ndim - 2) + [(0, 16), (0, 0)])
    row = lax.broadcasted_iota(jnp.int32, padded.shape, padded.ndim - 2)
    return jnp.where(row < rows, padded * jnp.exp2(14.0 - power), power).astype(jnp.float16)


def unpack(packed):
    power = packed[..., -1:, :1].astype(jnp.float32)
    return packed[..., :-16, :].astype(jnp.float32) / jnp.exp2(14.0 - power), jnp.max(power)


def local(features, adj_blocks, positions, counts, w_in, w_out, cotangent):
    slots, size = adj_blocks.shape[:2]
    nodes_dev, width = features.shape
    planes = lax.axis_size(("x", "y"))
    out_blocks = lax.axis_size(ROW) * nodes_dev // size
    in_blocks = lax.axis_size(COL) * nodes_dev // size
    spans = tuple(lax.axis_size(axis) for axis in COL)
    here = jnp.stack([lax.axis_index(axis) for axis in COL]).astype(jnp.int32)
    per_group = in_blocks // spans[0]

    def forward(groups, name, earlier=()):
        return tile_product(
            functools.partial(forward_kernel, spans),
            counts,
            positions,
            here,
            adj_blocks,
            groups,
            [(out_blocks, size, width)],
            name,
            earlier,
        )[0]

    near_one = share(features, ("y", "zl"))
    groups_one = share_x(near_one.reshape(per_group, size, width))
    group_grad = lax.all_gather(after(cotangent, near_one), "core", axis=0)
    group_grad = lax.all_gather(group_grad, "zh", axis=0).reshape(out_blocks, size, -1)
    *partial_two, top = tile_product(
        functools.partial(backward_kernel, spans),
        counts,
        positions,
        here,
        adj_blocks,
        [group_grad],
        [(per_group, size, width)] * spans[0] + [(8, size)],
        "backward",
        groups_one[1:],
    )
    bound = 0.01953125 * out_blocks * size
    most = jnp.clip(jnp.max(top), 1e-30, 1e38 / bound) * bound
    power = jnp.ceil(jnp.log2(most)) + 1.0
    flat = [part.reshape(-1, width) for part in partial_two]
    packed = lax.optimization_barrier([pack(part, power) for part in flat[1:]])

    partial_one = forward(groups_one, "forward_one", [packed[0][:16].astype(jnp.float32)])
    sums_one = exchange(partial_one, ROW)
    s_one = jnp.sum(sums_one, axis=0).astype(jnp.bfloat16)
    hidden = jnp.maximum(jnp.dot(s_one, w_in, preferred_element_type=jnp.float32), 0.0).astype(
        jnp.bfloat16
    )
    class_rows = jnp.dot(hidden, w_out, preferred_element_type=jnp.float32).astype(jnp.bfloat16)

    total = flat[0]
    for d, part in enumerate(packed, 1):
        part, other = unpack(send_ahead(part, "x", d))
        total, power = total + part, jnp.maximum(power, other)
    packed = pack(total.reshape(per_group, size, width), power + 2.0)
    sums_two = jnp.sum(unpack(exchange(packed, ("y", "zl")))[0], axis=0)
    d_two = sums_two.astype(jnp.bfloat16)

    near_two = share(after(class_rows, d_two), ("y", "zl"))
    groups_two = share_x(near_two.reshape(per_group, size, width))
    partial_out = forward(groups_two, "forward_two")

    local_out = jnp.einsum("nh,nc->hc", hidden, d_two, preferred_element_type=jnp.float32)
    d_hidden = jnp.einsum("nc,hc->nh", d_two, w_out, preferred_element_type=jnp.float32)
    masked = jnp.where(hidden > 0, d_hidden, 0.0).astype(jnp.bfloat16)
    local_in = jnp.einsum("nf,nh->fh", s_one, masked, preferred_element_type=jnp.float32)

    classes = local_out.shape[1]
    halves = local_in.shape[1] // classes
    parts = [local_in[:, i * classes : (i + 1) * classes] for i in range(halves)]
    grads = jnp.concatenate(parts + [local_out], axis=0).reshape(planes, -1, classes)
    grads = jnp.sum(exchange(grads, ("x", "y")), axis=0)
    output = jnp.sum(exchange(partial_out, ROW), axis=0).astype(jnp.bfloat16)
    for axis in ("zl", "core"):
        grads = jnp.sum(lax.all_gather(grads, axis, axis=0), axis=0)
    grads = jnp.sum(lax.all_gather(after(grads, partial_out), "zh", axis=0), axis=0)
    grads = share(grads, ("x", "y")).reshape(-1, classes)
    rows_in = local_in.shape[0]
    grad_in = jnp.concatenate(
        [grads[i * rows_in : (i + 1) * rows_in] for i in range(halves)], axis=1
    )
    grad_out = grads[halves * rows_in :]
    return (output, grad_in, grad_out)


def build(mesh, split):
    cut = Mesh(mesh.devices.reshape(tuple(split.values())), tuple(split))
    placed = (
        P(ALL, None),
        P(ALL, None, None),
        P(ALL, None),
        P(ALL),
        P(),
        P(),
        P(ALL, None),
    )
    return jax.shard_map(
        local,
        mesh=cut,
        in_specs=placed,
        out_specs=(P(ALL, None), P(), P()),
        check_vma=False,
    )


def solution(mesh):
    return build(mesh, SPLIT)
```

time: 405 us -> 343 us (0.85)
  the two profiles are of different devices: /device:TPU:1 before, /device:TPU:8 now
where the time goes in v2:
time: 343 us; the launch traced here: 341 us
  blocking collectives  141 us (41%)
  waiting for transfers between devices  83.2 us (24%)
  starting transfers between devices  62.6 us (18%)
  Pallas kernels  23.5 us (7%)
  local copies, waits for them, and re-layouts  12.6 us (4%)
  other arithmetic  12.3 us (4%)
  between operations  4.47 us (1%)
    all_to_all x3, blocking collectives, exchange(): return lax.all_to_all(values, axes, 0, 0)  84.9 us
    all_to_all x4, waiting for transfers between devices, exchange(): return lax.all_to_all(values, axes, 0, 0)  74.6 us
    all_to_all x4, starting transfers between devices, exchange(): return lax.all_to_all(values, axes, 0, 0)  33.3 us
    ppermute x9, starting transfers between devices, send_ahead(): lax.ppermute(values, axes, [(i, (i + distance) % size) for i in range(siz...  29.4 us
    all_gather x1, blocking collectives, local(): lax.all_gather(group_grad, 'zh', axis=0).reshape(out_blocks, size, -1)  23.8 us
    pallas_call x3, Pallas kernels, tile_product(): pl.pallas_call(body, out_shape=outs, in_specs=[smem] * 3 + [pl.BlockSpec(...  19.4 us
    all_gather x1, blocking collectives, local(): lax.all_gather(after(grads, partial_out), 'zh', axis=0)  18.2 us
    all_gather x2, blocking collectives, local(): grads = jnp.sum(lax.all_gather(grads, axis, axis=0), axis=0)  12.2 us
  transfers between devices with their start and end apart: 13, of which 6 were waited for; matrix products, arithmetic and copies ran while one was open for 3% of the time, Pallas kernels for 2%

profile of v2, /device:TPU:8, one launch (start us, length us, event | category | flops | bytes accessed | tf_op | source)
XLA Modules:
  0.0 341.4 jit_solution(12260224546002376901)
XLA Ops:
  1.6 32.8 %all_to_all.35.earlier_ref.refs_2_ = bf16[24,128,128]{2,1,0:T(8,128)(2,1)S(1)} all-to-all(bf16[24,128,128]{2,1,0:T(8,128)(2,1)S(1)} %broadcast_in_dim.30), channel_id=1, replica_groups=mesh['zh'=4,'core'=2,'x'=4,'y'=8,'zl'=3] {'y','zl'}, dimensions={0} | all-to-all | bytes 1572864 | tf_op jit(solution)/shard_map/all_to_all | solution.py:121
  34.4 3.1 collective-permute-start
  37.5 4.6 %collective-permute-start.1 = (bf16[24,128,128]{2,1,0:T(8,128)(2,1)S(1)}, bf16[24,128,128]{2,1,0:T(8,128)(2,1)}, u32[]{:S(2)}, u32[]{:S(2)}) collective-permute-start(bf16[24,128,128]{2,1,0:T(8,128)(2,1)S(1)} %all_to_all.35.earlier_ref.refs_2_), channel_id=1, source_target_pairs={{0,48},{24,72},{48,0},{72,24},{1,49},{25,73},{49,1},{73,25},{2,50}... | collective-permute-start | bytes 2359304 | tf_op jit(solution)/shard_map/ppermute | solution.py:126
  42.1 3.3 collective-permute-start.2
  49.6 23.8 %all-gather.1.refs_4_ = bf16[8,128,128]{2,1,0:T(8,128)(2,1)S(1)} all-gather(bf16[2,128,128]{2,1,0:T(8,128)(2,1)S(1)} %bitcast.43), channel_id=3, replica_groups=mesh['zh'=4,'core'=2,'x'=4,'y'=8,'zl'=3] {'zh'}, dimensions={0}, use_global_device_ids=true | all-gather | bytes 327680 | tf_op jit(solution)/shard_map/all_gather | solution.py:176
  74.4 7.2 %backward.1 = (f32[24,128,128]{2,1,0:T(8,128)S(1)}, f32[24,128,128]{2,1,0:T(8,128)S(1)}, f32[24,128,128]{2,1,0:T(8,128)S(1)}, f32[24,128,128]{2,1,0:T(8,128)S(1)}, f32[8,128]{1,0:T(8,128)S(1)}) custom-call(s32[1]{0:T(128)S(6)} %copy.13.count_ref, s32[1,48]{1,0:T(1,128)S(1)} %copy-done.9, s32[3]{0:T(128)S(1)} %pad_add_fusion.here_ref, ...), custom_call_target="tpu_custom_call" | custom-call | flops 1 | bytes 1 | tf_op jit(solution)/shard_map/backward/pallas_call | solution.py:107
  87.5 4.3 %select_convert_fusion.1 = (f16[3088,128]{1,0:T(8,128)(2,1)}, f16[3088,128]{1,0:T(8,128)(2,1)}, f16[3088,128]{1,0:T(8,128)(2,1)}) fusion(f32[3072,128]{1,0:T(8,128)} %bitcast.40, f32[]{:T(128)S(6)} %add.23, f32[]{:T(128)S(6)} %exp2.41, pred[3088]{0:T(1024)(128)(4,1)S(1)} %iota_compare_fusion, f32[3072,128]{1,0:T(8,128)} %bitcast.39, f32[3072,128]{1,0:T(8,128)} %bitcast.38), kind=kLoop, calls=%fused_computation.1 | loop fusion | flops 3557376 | bytes 7093272 | tf_op jit(solution)/shard_map/convert_element_type | solution.py:142
  96.6 4.6 %collective-permute-start.5 = (f16[3088,128]{1,0:T(8,128)(2,1)}, f16[3088,128]{1,0:T(8,128)(2,1)}, u32[]{:S(2)}, u32[]{:S(2)}) collective-permute-start(f16[3088,128]{1,0:T(8,128)(2,1)} %get-tuple-element.18), channel_id=1, source_target_pairs={{0,72},{24,0},{48,24},{72,48},{1,73},{25,1},{49,25},{73,49},{2,74}... | collective-permute-start | bytes 2371592 | tf_op jit(solution)/shard_map/ppermute | solution.py:126
  101.9 6.5 %forward_one.1 = f32[8,128,128]{2,1,0:T(8,128)} custom-call(s32[1]{0:T(128)S(6)} %copy.13.count_ref, s32[1,48]{1,0:T(1,128)S(1)} %copy-done.9, s32[3]{0:T(128)S(1)} %pad_add_fusion.here_ref, f32[16,128]{1,0:T(8,128)S(1)} %slice_convert_fusion.refs_0_, bf16[48,128,128]{2,1,0:T(8,128)(2,1)S(1)} %copy-done.1, bf16[24,128,128]{2,1,0:T(8,128)(2,1)S(1)} %copy-done.3, ...), custom_call_target="tpu_custom_call" | custom-call | flops 1 | bytes 1 | tf_op jit(solution)/shard_map/forward_one/pallas_call | solution.py:107
  108.4 12.7 %all-to-all-start.1 = ((f32[8,128,128]{2,1,0:T(8,128)}), f32[8,128,128]{2,1,0:T(8,128)S(1)}, u32[]{:S(2)}, u32[]{:S(2)}) async-start(f32[8,128,128]{2,1,0:T(8,128)} %forward_one.1), calls=%async_computation.1 | async-start | bytes 1048576 | tf_op jit(solution)/shard_map/all_to_all | solution.py:121
  121.1 7.7 %collective-permute-done.3 = f16[3088,128]{1,0:T(8,128)(2,1)} collective-permute-done((f16[3088,128]{1,0:T(8,128)(2,1)}, f16[3088,128]{1,0:T(8,128)(2,1)}, u32[]{:S(2)}, u32[]{:S(2)}) %collective-permute-start.3) | collective-permute-done | bytes 790560 | tf_op jit(solution)/shard_map/ppermute | solution.py:126
  138.3 6.5 %all-to-all-done.1 = f32[8,128,128]{2,1,0:T(8,128)S(1)} async-done(((f32[8,128,128]{2,1,0:T(8,128)}), f32[8,128,128]{2,1,0:T(8,128)S(1)}, u32[]{:S(2)}, u32[]{:S(2)}) %all-to-all-start.1) | async-done | bytes 524320 | tf_op jit(solution)/shard_map/all_to_all | solution.py:121
  144.8 9.2 %all-to-all-start.2 = ((f16[24,144,128]{2,1,0:T(8,128)(2,1)}), f16[24,144,128]{2,1,0:T(8,128)(2,1)S(1)}, u32[]{:S(2)}, u32[]{:S(2)}) async-start(f16[24,144,128]{2,1,0:T(8,128)(2,1)} %select_convert_fusion), calls=%async_computation.2 | async-start | bytes 1769472 | tf_op jit(solution)/shard_map/all_to_all | solution.py:121
  155.0 22.6 %all-to-all-done.2 = f16[24,144,128]{2,1,0:T(8,128)(2,1)S(1)} async-done(((f16[24,144,128]{2,1,0:T(8,128)(2,1)}), f16[24,144,128]{2,1,0:T(8,128)(2,1)S(1)}, u32[]{:S(2)}, u32[]{:S(2)}) %all-to-all-start.2) | async-done | bytes 884768 | tf_op jit(solution)/shard_map/all_to_all | solution.py:121
  181.8 5.7 %all-to-all-start.3 = ((bf16[24,128,128]{2,1,0:T(8,128)(2,1)}), bf16[24,128,128]{2,1,0:T(8,128)(2,1)S(1)}, u32[]{:S(2)}, u32[]{:S(2)}) async-start(bf16[24,128,128]{2,1,0:T(8,128)(2,1)} %broadcast_in_dim.33), calls=%async_computation.3 | async-start | bytes 1572864 | tf_op jit(solution)/shard_map/all_to_all | solution.py:121
  188.0 20.7 %all-to-all-done.3.refs_1_ = bf16[24,128,128]{2,1,0:T(8,128)(2,1)S(1)} async-done(((bf16[24,128,128]{2,1,0:T(8,128)(2,1)}), bf16[24,128,128]{2,1,0:T(8,128)(2,1)S(1)}, u32[]{:S(2)}, u32[]{:S(2)}) %all-to-all-start.3) | async-done | bytes 786464 | tf_op jit(solution)/shard_map/all_to_all | solution.py:121
  212.6 5.0 %collective-permute-start.8 = (bf16[24,128,128]{2,1,0:T(8,128)(2,1)S(1)}, bf16[24,128,128]{2,1,0:T(8,128)(2,1)}, u32[]{:S(2)}, u32[]{:S(2)}) collective-permute-start(bf16[24,128,128]{2,1,0:T(8,128)(2,1)S(1)} %all-to-all-done.3.refs_1_), channel_id=1, source_target_pairs={{0,72},{24,0},{48,24},{72,48},{1,73},{25,1},{49,25},{73,49},{2,74}... | collective-permute-start | bytes 2359304 | tf_op jit(solution)/shard_map/ppermute | solution.py:126
  217.7 34.2 %all_to_all.36 = f32[32,16,128]{2,1,0:T(8,128)S(1)} all-to-all(f32[32,16,128]{2,1,0:T(8,128)S(1)} %bitcast.42), channel_id=1, replica_groups=mesh['zh'=4,'core'=2,'x'=4,'y'=8,'zl'=3] {'x','y'}, dimensions={0} | all-to-all | bytes 524288 | tf_op jit(solution)/shard_map/all_to_all | solution.py:121
  252.0 10.4 %all-gather.2 = f32[48,128]{1,0:T(8,128)S(1)} all-gather(f32[16,128]{1,0:T(8,128)S(1)} %reduce_sum.66), channel_id=4, replica_groups=mesh['zh'=4,'core'=2,'x'=4,'y'=8,'zl'=3] {'zl'}, dimensions={0}, use_global_device_ids=true | all-gather | bytes 32768 | tf_op jit(solution)/shard_map/all_gather | solution.py:226
  264.8 5.7 %forward_two.1.earlier_ref = f32[8,128,128]{2,1,0:T(8,128)S(1)} custom-call(s32[1]{0:T(128)S(6)} %copy.13.count_ref, s32[1,48]{1,0:T(1,128)S(1)} %copy-done.9, s32[3]{0:T(128)S(1)} %pad_add_fusion.here_ref, bf16[48,128,128]{2,1,0:T(8,128)(2,1)S(1)} %copy-done.1, bf16[24,128,128]{2,1,0:T(8,128)(2,1)S(1)} %all-to-all-done.3.refs_1_, ...), custom_call_target="tpu_custom_call" | custom-call | flops 1 | bytes 1 | tf_op jit(solution)/shard_map/forward_two/pallas_call | solution.py:107
  272.6 18.2 %all-gather.4 = f32[64,128]{1,0:T(8,128)S(1)} all-gather(f32[16,128]{1,0:T(8,128)} %after.5), channel_id=6, replica_groups=mesh['zh'=4,'core'=2,'x'=4,'y'=8,'zl'=3] {'zh'}, dimensions={0}, use_global_device_ids=true | all-gather | bytes 40960 | tf_op jit(solution)/shard_map/all_gather | solution.py:227
  290.9 17.9 %all_to_all.37 = f32[32,16,128]{2,1,0:T(8,128)S(1)} all-to-all(f32[32,16,128]{2,1,0:T(8,128)S(1)} %broadcast_in_dim.34), channel_id=1, replica_groups=mesh['zh'=4,'core'=2,'x'=4,'y'=8,'zl'=3] {'x','y'}, dimensions={0} | all-to-all | bytes 524288 | tf_op jit(solution)/shard_map/all_to_all | solution.py:121
  308.8 5.7 %all-to-all-start.4 = ((f32[8,128,128]{2,1,0:T(8,128)}), f32[8,128,128]{2,1,0:T(8,128)S(1)}, u32[]{:S(2)}, u32[]{:S(2)}) async-start(f32[8,128,128]{2,1,0:T(8,128)} %copy-done.4), calls=%async_computation.4 | async-start | bytes 1048576 | tf_op jit(solution)/shard_map/all_to_all | solution.py:121
  315.9 24.8 %all-to-all-done.4 = f32[8,128,128]{2,1,0:T(8,128)S(1)} async-done(((f32[8,128,128]{2,1,0:T(8,128)}), f32[8,128,128]{2,1,0:T(8,128)S(1)}, u32[]{:S(2)}, u32[]{:S(2)}) %all-to-all-start.4) | async-done | bytes 524320 | tf_op jit(solution)/shard_map/all_to_all | solution.py:121
  (73 shorter events, 39.6 us)
Async XLA Ops:
  0.6 153.6 %copy-start = (bf16[256,128]{1,0:T(8,128)(2,1)S(1)}, bf16[256,128]{1,0:T(8,128)(2,1)}, u32[]{:S(2)}) copy-start(bf16[256,128]{1,0:T(8,128)(2,1)} %param.12) | copy-start | bytes 196612
  1.6 72.8 %copy-start.1 = (bf16[48,128,128]{2,1,0:T(8,128)(2,1)S(1)}, bf16[48,128,128]{2,1,0:T(8,128)(2,1)}, u32[]{:S(2)}) copy-start(bf16[48,128,128]{2,1,0:T(8,128)(2,1)} %refs_0_.1) | copy-start | bytes 4718596
  1.6 72.8 %copy-start.9 = (s32[1,48]{1,0:T(1,128)S(1)}, s32[1,48]{1,0:T(1,128)}, u32[]{:S(2)}) copy-start(s32[1,48]{1,0:T(1,128)} %place_ref.5) | copy-start | bytes 580
  34.4 11.8 %copy-start.2 = (bf16[24,128,128]{2,1,0:T(8,128)(2,1)}, bf16[24,128,128]{2,1,0:T(8,128)(2,1)S(1)}, u32[]{:S(2)}) copy-start(bf16[24,128,128]{2,1,0:T(8,128)(2,1)S(1)} %all_to_all.35.earlier_ref.refs_2_) | copy-start | bytes 2359300
  34.4 39.1 %collective-permute-start = (bf16[24,128,128]{2,1,0:T(8,128)(2,1)S(1)}, bf16[24,128,128]{2,1,0:T(8,128)(2,1)S(1)}, u32[]{:S(2)}, u32[]{:S(2)}) collective-permute-start(bf16[24,128,128]{2,1,0:T(8,128)(2,1)S(1)} %all_to_all.35.earlier_ref.refs_2_), channel_id=1, source_target_pairs={{0,24},{24,48},{48,72},{72,0},{1,25},{25,49},{49,73},{73,1},{2,26}... | collective-permute-start | bytes 2359304 | tf_op jit(solution)/shard_map/ppermute | solution.py:126
  37.5 36.0 %collective-permute-start.1 = (bf16[24,128,128]{2,1,0:T(8,128)(2,1)S(1)}, bf16[24,128,128]{2,1,0:T(8,128)(2,1)}, u32[]{:S(2)}, u32[]{:S(2)}) collective-permute-start(bf16[24,128,128]{2,1,0:T(8,128)(2,1)S(1)} %all_to_all.35.earlier_ref.refs_2_), channel_id=1, source_target_pairs={{0,48},{24,72},{48,0},{72,24},{1,49},{25,73},{49,1},{73,25},{2,50}... | collective-permute-start | bytes 2359304 | tf_op jit(solution)/shard_map/ppermute | solution.py:126
  42.1 32.2 %collective-permute-start.2 = (bf16[24,128,128]{2,1,0:T(8,128)(2,1)S(1)}, bf16[24,128,128]{2,1,0:T(8,128)(2,1)}, u32[]{:S(2)}, u32[]{:S(2)}) collective-permute-start(bf16[24,128,128]{2,1,0:T(8,128)(2,1)S(1)} %all_to_all.35.earlier_ref.refs_2_), channel_id=1, source_target_pairs={{0,72},{24,0},{48,24},{72,48},{1,73},{25,1},{49,25},{73,49},{2,74}... | collective-permute-start | bytes 2359304 | tf_op jit(solution)/shard_map/ppermute | solution.py:126
  81.6 1.1 copy-start.5
  82.7 1.2 copy-start.6
  83.9 1.2 copy-start.7
  85.0 1.1 copy-start.8
  87.5 14.4 %copy-start.3 = (bf16[24,128,128]{2,1,0:T(8,128)(2,1)S(1)}, bf16[24,128,128]{2,1,0:T(8,128)(2,1)}, u32[]{:S(2)}) copy-start(bf16[24,128,128]{2,1,0:T(8,128)(2,1)} %copy-done.2) | copy-start | bytes 2359300
  91.9 37.0 %collective-permute-start.3 = (f16[3088,128]{1,0:T(8,128)(2,1)}, f16[3088,128]{1,0:T(8,128)(2,1)}, u32[]{:S(2)}, u32[]{:S(2)}) collective-permute-start(f16[3088,128]{1,0:T(8,128)(2,1)} %get-tuple-element.15), channel_id=1, source_target_pairs={{0,24},{24,48},{48,72},{72,0},{1,25},{25,49},{49,73},{73,1},{2,26}... | collective-permute-start | bytes 2371592 | tf_op jit(solution)/shard_map/ppermute | solution.py:126
  94.7 36.0 %collective-permute-start.4 = (f16[3088,128]{1,0:T(8,128)(2,1)}, f16[3088,128]{1,0:T(8,128)(2,1)}, u32[]{:S(2)}, u32[]{:S(2)}) collective-permute-start(f16[3088,128]{1,0:T(8,128)(2,1)} %get-tuple-element.17), channel_id=1, source_target_pairs={{0,48},{24,72},{48,0},{72,24},{1,49},{25,73},{49,1},{73,25},{2,50}... | collective-permute-start | bytes 2371592 | tf_op jit(solution)/shard_map/ppermute | solution.py:126
  96.6 35.9 %collective-permute-start.5 = (f16[3088,128]{1,0:T(8,128)(2,1)}, f16[3088,128]{1,0:T(8,128)(2,1)}, u32[]{:S(2)}, u32[]{:S(2)}) collective-permute-start(f16[3088,128]{1,0:T(8,128)(2,1)} %get-tuple-element.18), channel_id=1, source_target_pairs={{0,72},{24,0},{48,24},{72,48},{1,73},{25,1},{49,25},{73,49},{2,74}... | collective-permute-start | bytes 2371592 | tf_op jit(solution)/shard_map/ppermute | solution.py:126
  108.4 36.4 %all-to-all-start.1 = ((f32[8,128,128]{2,1,0:T(8,128)}), f32[8,128,128]{2,1,0:T(8,128)S(1)}, u32[]{:S(2)}, u32[]{:S(2)}) async-start(f32[8,128,128]{2,1,0:T(8,128)} %forward_one.1), calls=%async_computation.1 | async-start | bytes 1048576 | tf_op jit(solution)/shard_map/all_to_all | solution.py:121
  138.3 15.7 %copy-start.11 = (bf16[128,256]{1,0:T(8,128)(2,1)S(1)}, bf16[128,256]{1,0:T(8,128)(2,1)}, u32[]{:S(2)}) copy-start(bf16[128,256]{1,0:T(8,128)(2,1)} %param.11) | copy-start | bytes 196612
  144.8 32.8 %all-to-all-start.2 = ((f16[24,144,128]{2,1,0:T(8,128)(2,1)}), f16[24,144,128]{2,1,0:T(8,128)(2,1)S(1)}, u32[]{:S(2)}, u32[]{:S(2)}) async-start(f16[24,144,128]{2,1,0:T(8,128)(2,1)} %select_convert_fusion), calls=%async_computation.2 | async-start | bytes 1769472 | tf_op jit(solution)/shard_map/all_to_all | solution.py:121
  178.6 8.9 %copy-start.10 = (bf16[128,128]{1,0:T(8,128)(2,1)S(1)}, bf16[128,128]{1,0:T(8,128)(2,1)}, u32[]{:S(2)}) copy-start(bf16[128,128]{1,0:T(8,128)(2,1)} %fusion.2.earlier_ref) | copy-start | bytes 98308
  181.8 26.9 %all-to-all-start.3 = ((bf16[24,128,128]{2,1,0:T(8,128)(2,1)}), bf16[24,128,128]{2,1,0:T(8,128)(2,1)S(1)}, u32[]{:S(2)}, u32[]{:S(2)}) async-start(bf16[24,128,128]{2,1,0:T(8,128)(2,1)} %broadcast_in_dim.33), calls=%async_computation.3 | async-start | bytes 1572864 | tf_op jit(solution)/shard_map/all_to_all | solution.py:121
  208.7 56.1 %collective-permute-start.6 = (bf16[24,128,128]{2,1,0:T(8,128)(2,1)S(1)}, bf16[24,128,128]{2,1,0:T(8,128)(2,1)S(1)}, u32[]{:S(2)}, u32[]{:S(2)}) collective-permute-start(bf16[24,128,128]{2,1,0:T(8,128)(2,1)S(1)} %all-to-all-done.3.refs_1_), channel_id=1, source_target_pairs={{0,24},{24,48},{48,72},{72,0},{1,25},{25,49},{49,73},{73,1},{2,26}... | collective-permute-start | bytes 2359304 | tf_op jit(solution)/shard_map/ppermute | solution.py:126
  210.6 54.2 %collective-permute-start.7 = (bf16[24,128,128]{2,1,0:T(8,128)(2,1)S(1)}, bf16[24,128,128]{2,1,0:T(8,128)(2,1)}, u32[]{:S(2)}, u32[]{:S(2)}) collective-permute-start(bf16[24,128,128]{2,1,0:T(8,128)(2,1)S(1)} %all-to-all-done.3.refs_1_), channel_id=1, source_target_pairs={{0,48},{24,72},{48,0},{72,24},{1,49},{25,73},{49,1},{73,25},{2,50}... | collective-permute-start | bytes 2359304 | tf_op jit(solution)/shard_map/ppermute | solution.py:126
  212.6 52.1 %collective-permute-start.8 = (bf16[24,128,128]{2,1,0:T(8,128)(2,1)S(1)}, bf16[24,128,128]{2,1,0:T(8,128)(2,1)}, u32[]{:S(2)}, u32[]{:S(2)}) collective-permute-start(bf16[24,128,128]{2,1,0:T(8,128)(2,1)S(1)} %all-to-all-done.3.refs_1_), channel_id=1, source_target_pairs={{0,72},{24,0},{48,24},{72,48},{1,73},{25,1},{49,25},{73,49},{2,74}... | collective-permute-start | bytes 2359304 | tf_op jit(solution)/shard_map/ppermute | solution.py:126
  308.8 31.9 %all-to-all-start.4 = ((f32[8,128,128]{2,1,0:T(8,128)}), f32[8,128,128]{2,1,0:T(8,128)S(1)}, u32[]{:S(2)}, u32[]{:S(2)}) async-start(f32[8,128,128]{2,1,0:T(8,128)} %copy-done.4), calls=%async_computation.4 | async-start | bytes 1048576 | tf_op jit(solution)/shard_map/all_to_all | solution.py:121
  (1 other events, 0.8 us)

commit v3 on v2

--- a/solution.py
+++ b/solution.py
@@ -142,9 +142,9 @@
     return jnp.where(row < rows, padded * jnp.exp2(14.0 - power), power).astype(jnp.float16)
 
 
-def unpack(packed):
+def unpack(packed, base=14.0):
     power = packed[..., -1:, :1].astype(jnp.float32)
-    return packed[..., :-16, :].astype(jnp.float32) / jnp.exp2(14.0 - power), jnp.max(power)
+    return packed[..., :-16, :].astype(jnp.float32) / jnp.exp2(base - power), jnp.max(power)
 
 
 def local(features, adj_blocks, positions, counts, w_in, w_out, cotangent):
@@ -183,33 +183,34 @@
         [group_grad],
         [(per_group, size, width)] * spans[0] + [(8, size)],
         "backward",
-        groups_one[1:],
-    )
+    )
+    partial_one = forward(groups_one, "forward_one", [group_grad])
+    sums_one = exchange(partial_one, ROW)
+    s_one = jnp.sum(sums_one, axis=0).astype(jnp.bfloat16)
+    hidden = jnp.maximum(jnp.dot(s_one, w_in, preferred_element_type=jnp.float32), 0.0).astype(
+        jnp.bfloat16
+    )
+    class_rows = jnp.dot(hidden, w_out, preferred_element_type=jnp.float32).astype(jnp.bfloat16)
+
+    top = after(top, class_rows)
     bound = 0.01953125 * out_blocks * size
     most = jnp.clip(jnp.max(top), 1e-30, 1e38 / bound) * bound
     power = jnp.ceil(jnp.log2(most)) + 1.0
     flat = [part.reshape(-1, width) for part in partial_two]
     packed = lax.optimization_barrier([pack(part, power) for part in flat[1:]])
 
-    partial_one = forward(groups_one, "forward_one", [packed[0][:16].astype(jnp.float32)])
-    sums_one = exchange(partial_one, ROW)
-    s_one = jnp.sum(sums_one, axis=0).astype(jnp.bfloat16)
-    hidden = jnp.maximum(jnp.dot(s_one, w_in, preferred_element_type=jnp.float32), 0.0).astype(
-        jnp.bfloat16
-    )
-    class_rows = jnp.dot(hidden, w_out, preferred_element_type=jnp.float32).astype(jnp.bfloat16)
-
+    near_two = lax.all_gather(lax.all_gather(class_rows, "zl", axis=0), "y", axis=0)
+    groups_two = share_x(near_two.reshape(per_group, size, width))
+    partial_out = forward(groups_two, "forward_two")
+
+    base = after(jnp.full(top.shape, 14.0, jnp.float32), near_two)[0, 0]
     total = flat[0]
     for d, part in enumerate(packed, 1):
-        part, other = unpack(send_ahead(part, "x", d))
+        part, other = unpack(send_ahead(part, "x", d), base)
         total, power = total + part, jnp.maximum(power, other)
     packed = pack(total.reshape(per_group, size, width), power + 2.0)
     sums_two = jnp.sum(unpack(exchange(packed, ("y", "zl")))[0], axis=0)
     d_two = sums_two.astype(jnp.bfloat16)
-
-    near_two = share(after(class_rows, d_two), ("y", "zl"))
-    groups_two = share_x(near_two.reshape(per_group, size, width))
-    partial_out = forward(groups_two, "forward_two")
 
     local_out = jnp.einsum("nh,nc->hc", hidden, d_two, preferred_element_type=jnp.float32)
     d_hidden = jnp.einsum("nc,hc->nh", d_two, w_out, preferred_element_type=jnp.float32)
@@ -222,9 +223,7 @@
     grads = jnp.concatenate(parts + [local_out], axis=0).reshape(planes, -1, classes)
     grads = jnp.sum(exchange(grads, ("x", "y")), axis=0)
     output = jnp.sum(exchange(partial_out, ROW), axis=0).astype(jnp.bfloat16)
-    for axis in ("zl", "core"):
-        grads = jnp.sum(lax.all_gather(grads, axis, axis=0), axis=0)
-    grads = jnp.sum(lax.all_gather(after(grads, partial_out), "zh", axis=0), axis=0)
+    grads = jnp.sum(share(after(grads, partial_out), ("zh", "core", "zl")), axis=0)
     grads = share(grads, ("x", "y")).reshape(-1, classes)
     rows_in = local_in.shape[0]
     grad_in = jnp.concatenate(

time: 343 us -> 317 us (0.924)
  the two profiles are of different devices: /device:TPU:8 before, /device:TPU:72 now
where the time goes in v3:
time: 317 us; the launch traced here: 316 us
  blocking collectives  113 us (36%)
  starting transfers between devices  78.4 us (25%)
  waiting for transfers between devices  77.5 us (24%)
  local copies, waits for them, and re-layouts  16 us (5%)
  other arithmetic  13.1 us (4%)
  Pallas kernels  10.3 us (3%)
  between operations  6.44 us (2%)
    all_to_all x5, waiting for transfers between devices, exchange(): return lax.all_to_all(values, axes, 0, 0)  65.3 us
    all_to_all x2, blocking collectives, exchange(): return lax.all_to_all(values, axes, 0, 0)  50.5 us
    all_to_all x5, starting transfers between devices, exchange(): return lax.all_to_all(values, axes, 0, 0)  47.1 us
    ppermute x9, starting transfers between devices, send_ahead(): lax.ppermute(values, axes, [(i, (i + distance) % size) for i in range(siz...  31.4 us
    all_gather x1, blocking collectives, local(): lax.all_gather(lax.all_gather(class_rows, 'zl', axis=0), 'y', axis=0)  26.7 us
    all_gather x1, blocking collectives, local(): lax.all_gather(group_grad, 'zh', axis=0).reshape(out_blocks, size, -1)  24 us
    ppermute x9, waiting for transfers between devices, send_ahead(): lax.ppermute(values, axes, [(i, (i + distance) % size) for i in range(siz...  12.2 us
    all_gather x1, blocking collectives, local(): lax.all_gather(class_rows, 'zl', axis=0)  9.42 us
  transfers between devices with their start and end apart: 14, of which 6 were waited for; matrix products, arithmetic and copies ran while one was open for 3% of the time, Pallas kernels for 2%

profile of v3, /device:TPU:72, one launch (start us, length us, event | category | flops | bytes accessed | tf_op | source)
XLA Modules:
  0.0 315.9 jit_solution(10882174368085247024)
XLA Ops:
  1.6 31.9 %all_to_all.35.earlier_ref.refs_2_ = bf16[24,128,128]{2,1,0:T(8,128)(2,1)S(1)} all-to-all(bf16[24,128,128]{2,1,0:T(8,128)(2,1)S(1)} %broadcast_in_dim.33), channel_id=1, replica_groups=mesh['zh'=4,'core'=2,'x'=4,'y'=8,'zl'=3] {'y','zl'}, dimensions={0} | all-to-all | bytes 1572864 | tf_op jit(solution)/shard_map/all_to_all | solution.py:121
  33.5 3.4 %collective-permute-start = (bf16[24,128,128]{2,1,0:T(8,128)(2,1)S(1)}, bf16[24,128,128]{2,1,0:T(8,128)(2,1)S(1)}, u32[]{:S(2)}, u32[]{:S(2)}) collective-permute-start(bf16[24,128,128]{2,1,0:T(8,128)(2,1)S(1)} %all_to_all.35.earlier_ref.refs_2_), channel_id=1, source_target_pairs={{0,24},{24,48},{48,72},{72,0},{1,25},{25,49},{49,73},{73,1},{2,26}... | collective-permute-start | bytes 2359304 | tf_op jit(solution)/shard_map/ppermute | solution.py:126
  36.9 4.6 %collective-permute-start.1 = (bf16[24,128,128]{2,1,0:T(8,128)(2,1)S(1)}, bf16[24,128,128]{2,1,0:T(8,128)(2,1)}, u32[]{:S(2)}, u32[]{:S(2)}) collective-permute-start(bf16[24,128,128]{2,1,0:T(8,128)(2,1)S(1)} %all_to_all.35.earlier_ref.refs_2_), channel_id=1, source_target_pairs={{0,48},{24,72},{48,0},{72,24},{1,49},{25,73},{49,1},{73,25},{2,50}... | collective-permute-start | bytes 2359304 | tf_op jit(solution)/shard_map/ppermute | solution.py:126
  41.5 3.3 %collective-permute-start.2 = (bf16[24,128,128]{2,1,0:T(8,128)(2,1)S(1)}, bf16[24,128,128]{2,1,0:T(8,128)(2,1)}, u32[]{:S(2)}, u32[]{:S(2)}) collective-permute-start(bf16[24,128,128]{2,1,0:T(8,128)(2,1)S(1)} %all_to_all.35.earlier_ref.refs_2_), channel_id=1, source_target_pairs={{0,72},{24,0},{48,24},{72,48},{1,73},{25,1},{49,25},{73,49},{2,74}... | collective-permute-start | bytes 2359304 | tf_op jit(solution)/shard_map/ppermute | solution.py:126
  49.1 24.0 %all-gather.1.refs_0_.refs_1_ = bf16[8,128,128]{2,1,0:T(8,128)(2,1)S(1)} all-gather(bf16[2,128,128]{2,1,0:T(8,128)(2,1)S(1)} %bitcast.44), channel_id=3, replica_groups=mesh['zh'=4,'core'=2,'x'=4,'y'=8,'zl'=3] {'zh'}, dimensions={0}, use_global_device_ids=true | all-gather | bytes 327680 | tf_op jit(solution)/shard_map/all_gather | solution.py:176
  76.6 15.7 %all-to-all-start.1 = ((f32[8,128,128]{2,1,0:T(8,128)}), f32[8,128,128]{2,1,0:T(8,128)S(1)}, u32[]{:S(2)}, u32[]{:S(2)}) async-start(f32[8,128,128]{2,1,0:T(8,128)} %forward_one.1), calls=%async_computation.1 | async-start | bytes 1048576 | tf_op jit(solution)/shard_map/all_to_all | solution.py:121
  98.1 20.6 %all-to-all-done.1 = f32[8,128,128]{2,1,0:T(8,128)S(1)} async-done(((f32[8,128,128]{2,1,0:T(8,128)}), f32[8,128,128]{2,1,0:T(8,128)S(1)}, u32[]{:S(2)}, u32[]{:S(2)}) %all-to-all-start.1) | async-done | bytes 524320 | tf_op jit(solution)/shard_map/all_to_all | solution.py:121
  123.1 4.3 %select_convert_fusion.1 = (f16[3088,128]{1,0:T(8,128)(2,1)}, f16[3088,128]{1,0:T(8,128)(2,1)}, f16[3088,128]{1,0:T(8,128)(2,1)}) fusion(f32[3072,128]{1,0:T(8,128)} %bitcast.40, f32[]{:T(128)S(6)} %add.23, f32[]{:T(128)S(6)} %exp2.41, pred[3088]{0:T(1024)(128)(4,1)S(1)} %iota_compare_fusion, f32[3072,128]{1,0:T(8,128)} %bitcast.39, f32[3072,128]{1,0:T(8,128)} %bitcast.38), kind=kLoop, calls=%fused_computation.1 | loop fusion | flops 3557376 | bytes 7093272 | tf_op jit(solution)/shard_map/convert_element_type | solution.py:142
  127.3 4.5 %collective-permute-start.6 = (f16[3088,128]{1,0:T(8,128)(2,1)}, f16[3088,128]{1,0:T(8,128)(2,1)}, u32[]{:S(2)}, u32[]{:S(2)}) collective-permute-start(f16[3088,128]{1,0:T(8,128)(2,1)} %get-tuple-element.16), channel_id=1, source_target_pairs={{0,24},{24,48},{48,72},{72,0},{1,25},{25,49},{49,73},{73,1},{2,26}... | collective-permute-start | bytes 2371592 | tf_op jit(solution)/shard_map/ppermute | solution.py:126
  134.9 3.4 %collective-permute-start.8 = (f16[3088,128]{1,0:T(8,128)(2,1)}, f16[3088,128]{1,0:T(8,128)(2,1)}, u32[]{:S(2)}, u32[]{:S(2)}) collective-permute-start(f16[3088,128]{1,0:T(8,128)(2,1)} %get-tuple-element.18), channel_id=1, source_target_pairs={{0,72},{24,0},{48,24},{72,48},{1,73},{25,1},{49,25},{73,49},{2,74}... | collective-permute-start | bytes 2371592 | tf_op jit(solution)/shard_map/ppermute | solution.py:126
  138.4 9.4 %all-gather.2 = bf16[384,128]{1,0:T(8,128)(2,1)S(1)} all-gather(bf16[128,128]{1,0:T(8,128)(2,1)S(1)} %copy-done.13), channel_id=4, replica_groups=mesh['zh'=4,'core'=2,'x'=4,'y'=8,'zl'=3] {'zl'}, dimensions={0}, use_global_device_ids=true | all-gather | bytes 131072 | tf_op jit(solution)/shard_map/all_gather | solution.py:202
  147.8 26.7 %all-gather.3.refs_1_ = bf16[24,128,128]{2,1,0:T(8,128)(2,1)} all-gather(bf16[3,128,128]{2,1,0:T(8,128)(2,1)S(1)} %bitcast.43), channel_id=5, replica_groups=mesh['zh'=4,'core'=2,'x'=4,'y'=8,'zl'=3] {'y'}, dimensions={0}, use_global_device_ids=true | all-gather | bytes 884736 | tf_op jit(solution)/shard_map/all_gather | solution.py:202
  188.7 8.4 %all-to-all-start.3 = ((f16[24,144,128]{2,1,0:T(8,128)(2,1)}), f16[24,144,128]{2,1,0:T(8,128)(2,1)}, u32[]{:S(2)}, u32[]{:S(2)}) async-start(f16[24,144,128]{2,1,0:T(8,128)(2,1)} %select_convert_fusion), calls=%async_computation.3 | async-start | bytes 1769472 | tf_op jit(solution)/shard_map/all_to_all | solution.py:121
  199.4 3.1 collective-permute-start.4
  202.5 3.6 %collective-permute-start.5 = (bf16[24,128,128]{2,1,0:T(8,128)(2,1)S(1)}, bf16[24,128,128]{2,1,0:T(8,128)(2,1)}, u32[]{:S(2)}, u32[]{:S(2)}) collective-permute-start(bf16[24,128,128]{2,1,0:T(8,128)(2,1)S(1)} %copy-done.2), channel_id=1, source_target_pairs={{0,72},{24,0},{48,24},{72,48},{1,73},{25,1},{49,25},{73,49},{2,74}... | collective-permute-start | bytes 2359304 | tf_op jit(solution)/shard_map/ppermute | solution.py:126
  206.1 8.2 %all-to-all-done.3 = f16[24,144,128]{2,1,0:T(8,128)(2,1)} async-done(((f16[24,144,128]{2,1,0:T(8,128)(2,1)}), f16[24,144,128]{2,1,0:T(8,128)(2,1)}, u32[]{:S(2)}, u32[]{:S(2)}) %all-to-all-start.3) | async-done | bytes 884768 | tf_op jit(solution)/shard_map/all_to_all | solution.py:121
  217.9 4.4 %all-to-all-start.4 = ((f32[32,16,128]{2,1,0:T(8,128)}), f32[32,16,128]{2,1,0:T(8,128)S(1)}, u32[]{:S(2)}, u32[]{:S(2)}) async-start(f32[32,16,128]{2,1,0:T(8,128)} %bitcast.42), calls=%async_computation.4 | async-start | bytes 524288 | tf_op jit(solution)/shard_map/all_to_all | solution.py:121
  222.3 9.0 %collective-permute-done.3.refs_2_ = bf16[24,128,128]{2,1,0:T(8,128)(2,1)S(1)} collective-permute-done((bf16[24,128,128]{2,1,0:T(8,128)(2,1)S(1)}, bf16[24,128,128]{2,1,0:T(8,128)(2,1)S(1)}, u32[]{:S(2)}, u32[]{:S(2)}) %collective-permute-start.3) | collective-permute-done | bytes 786464 | tf_op jit(solution)/shard_map/ppermute | solution.py:126
  231.2 3.2 %collective-permute-done.5.refs_4_ = bf16[24,128,128]{2,1,0:T(8,128)(2,1)} collective-permute-done((bf16[24,128,128]{2,1,0:T(8,128)(2,1)S(1)}, bf16[24,128,128]{2,1,0:T(8,128)(2,1)}, u32[]{:S(2)}, u32[]{:S(2)}) %collective-permute-start.5) | collective-permute-done | bytes 786464 | tf_op jit(solution)/shard_map/ppermute | solution.py:126
  239.5 18.6 %all_to_all.36 = f32[24,16,128]{2,1,0:T(8,128)S(1)} all-to-all(f32[24,16,128]{2,1,0:T(8,128)S(1)} %broadcast_in_dim.37), channel_id=1, replica_groups=mesh['zh'=4,'core'=2,'x'=4,'y'=8,'zl'=3] {'zh','core','zl'}, dimensions={0} | all-to-all | bytes 393216 | tf_op jit(solution)/shard_map/all_to_all | solution.py:121
  258.1 5.5 %all-to-all-start.2 = ((f32[8,128,128]{2,1,0:T(8,128)}), f32[8,128,128]{2,1,0:T(8,128)S(1)}, u32[]{:S(2)}, u32[]{:S(2)}) async-start(f32[8,128,128]{2,1,0:T(8,128)} %copy-done.5), calls=%async_computation.2 | async-start | bytes 1048576 | tf_op jit(solution)/shard_map/all_to_all | solution.py:121
  264.3 25.0 %all-to-all-done.2 = f32[8,128,128]{2,1,0:T(8,128)S(1)} async-done(((f32[8,128,128]{2,1,0:T(8,128)}), f32[8,128,128]{2,1,0:T(8,128)S(1)}, u32[]{:S(2)}, u32[]{:S(2)}) %all-to-all-start.2) | async-done | bytes 524320 | tf_op jit(solution)/shard_map/all_to_all | solution.py:121
  289.3 13.0 %all-to-all-start.6 = ((f32[32,16,128]{2,1,0:T(8,128)}), f32[32,16,128]{2,1,0:T(8,128)S(1)}, u32[]{:S(2)}, u32[]{:S(2)}) async-start(f32[32,16,128]{2,1,0:T(8,128)} %broadcast_in_dim.38), calls=%async_computation.6 | async-start | bytes 524288 | tf_op jit(solution)/shard_map/all_to_all | solution.py:121
  302.9 11.6 %all-to-all-done.6 = f32[32,16,128]{2,1,0:T(8,128)S(1)} async-done(((f32[32,16,128]{2,1,0:T(8,128)}), f32[32,16,128]{2,1,0:T(8,128)S(1)}, u32[]{:S(2)}, u32[]{:S(2)}) %all-to-all-start.6) | async-done | bytes 262176 | tf_op jit(solution)/shard_map/all_to_all | solution.py:121
  (79 shorter events, 44.0 us)
Async XLA Ops:
  0.6 118.3 %copy-start = (bf16[256,128]{1,0:T(8,128)(2,1)S(1)}, bf16[256,128]{1,0:T(8,128)(2,1)}, u32[]{:S(2)}) copy-start(bf16[256,128]{1,0:T(8,128)(2,1)} %param.12) | copy-start | bytes 196612
  1.6 71.4 %copy-start.1 = (bf16[48,128,128]{2,1,0:T(8,128)(2,1)S(1)}, bf16[48,128,128]{2,1,0:T(8,128)(2,1)}, u32[]{:S(2)}) copy-start(bf16[48,128,128]{2,1,0:T(8,128)(2,1)} %refs_0_.3) | copy-start | bytes 4718596
  1.6 71.4 %copy-start.11 = (s32[1,48]{1,0:T(1,128)S(1)}, s32[1,48]{1,0:T(1,128)}, u32[]{:S(2)}) copy-start(s32[1,48]{1,0:T(1,128)} %place_ref.5) | copy-start | bytes 580
  33.5 12.1 %copy-start.3 = (bf16[24,128,128]{2,1,0:T(8,128)(2,1)}, bf16[24,128,128]{2,1,0:T(8,128)(2,1)S(1)}, u32[]{:S(2)}) copy-start(bf16[24,128,128]{2,1,0:T(8,128)(2,1)S(1)} %all_to_all.35.earlier_ref.refs_2_) | copy-start | bytes 2359300
  33.5 39.5 %collective-permute-start = (bf16[24,128,128]{2,1,0:T(8,128)(2,1)S(1)}, bf16[24,128,128]{2,1,0:T(8,128)(2,1)S(1)}, u32[]{:S(2)}, u32[]{:S(2)}) collective-permute-start(bf16[24,128,128]{2,1,0:T(8,128)(2,1)S(1)} %all_to_all.35.earlier_ref.refs_2_), channel_id=1, source_target_pairs={{0,24},{24,48},{48,72},{72,0},{1,25},{25,49},{49,73},{73,1},{2,26}... | collective-permute-start | bytes 2359304 | tf_op jit(solution)/shard_map/ppermute | solution.py:126
  36.9 36.1 %collective-permute-start.1 = (bf16[24,128,128]{2,1,0:T(8,128)(2,1)S(1)}, bf16[24,128,128]{2,1,0:T(8,128)(2,1)}, u32[]{:S(2)}, u32[]{:S(2)}) collective-permute-start(bf16[24,128,128]{2,1,0:T(8,128)(2,1)S(1)} %all_to_all.35.earlier_ref.refs_2_), channel_id=1, source_target_pairs={{0,48},{24,72},{48,0},{72,24},{1,49},{25,73},{49,1},{73,25},{2,50}... | collective-permute-start | bytes 2359304 | tf_op jit(solution)/shard_map/ppermute | solution.py:126
  41.5 31.5 %collective-permute-start.2 = (bf16[24,128,128]{2,1,0:T(8,128)(2,1)S(1)}, bf16[24,128,128]{2,1,0:T(8,128)(2,1)}, u32[]{:S(2)}, u32[]{:S(2)}) collective-permute-start(bf16[24,128,128]{2,1,0:T(8,128)(2,1)S(1)} %all_to_all.35.earlier_ref.refs_2_), channel_id=1, source_target_pairs={{0,72},{24,0},{48,24},{72,48},{1,73},{25,1},{49,25},{73,49},{2,74}... | collective-permute-start | bytes 2359304 | tf_op jit(solution)/shard_map/ppermute | solution.py:126
  76.6 42.3 %copy-start.14 = (bf16[128,256]{1,0:T(8,128)(2,1)S(1)}, bf16[128,256]{1,0:T(8,128)(2,1)}, u32[]{:S(2)}) copy-start(bf16[128,256]{1,0:T(8,128)(2,1)} %param.11) | copy-start | bytes 196612
  76.6 42.2 %all-to-all-start.1 = ((f32[8,128,128]{2,1,0:T(8,128)}), f32[8,128,128]{2,1,0:T(8,128)S(1)}, u32[]{:S(2)}, u32[]{:S(2)}) async-start(f32[8,128,128]{2,1,0:T(8,128)} %forward_one.1), calls=%async_computation.1 | async-start | bytes 1048576 | tf_op jit(solution)/shard_map/all_to_all | solution.py:121
  94.7 1.2 copy-start.8
  98.1 21.6 %copy-start.12 = (f32[8,128]{1,0:T(8,128)}, f32[8,128]{1,0:T(8,128)S(1)}, u32[]{:S(2)}) copy-start(f32[8,128]{1,0:T(8,128)S(1)} %get-tuple-element.13.values_ref) | copy-start | bytes 12292
  123.1 15.3 %copy-start.13 = (bf16[128,128]{1,0:T(8,128)(2,1)S(1)}, bf16[128,128]{1,0:T(8,128)(2,1)}, u32[]{:S(2)}) copy-start(bf16[128,128]{1,0:T(8,128)(2,1)} %convolution_convert_fusion.earlier_ref) | copy-start | bytes 98308
  127.3 57.9 %copy-start.7 = (f32[24,128,128]{2,1,0:T(8,128)S(1)}, f32[24,128,128]{2,1,0:T(8,128)}, u32[]{:S(2)}) copy-start(f32[24,128,128]{2,1,0:T(8,128)} %copy-done.6) | copy-start | bytes 4718596
  127.3 50.2 %collective-permute-start.6 = (f16[3088,128]{1,0:T(8,128)(2,1)}, f16[3088,128]{1,0:T(8,128)(2,1)}, u32[]{:S(2)}, u32[]{:S(2)}) collective-permute-start(f16[3088,128]{1,0:T(8,128)(2,1)} %get-tuple-element.16), channel_id=1, source_target_pairs={{0,24},{24,48},{48,72},{72,0},{1,25},{25,49},{49,73},{73,1},{2,26}... | collective-permute-start | bytes 2371592 | tf_op jit(solution)/shard_map/ppermute | solution.py:126
  131.9 47.6 %collective-permute-start.7 = (f16[3088,128]{1,0:T(8,128)(2,1)}, f16[3088,128]{1,0:T(8,128)(2,1)}, u32[]{:S(2)}, u32[]{:S(2)}) collective-permute-start(f16[3088,128]{1,0:T(8,128)(2,1)} %get-tuple-element.17), channel_id=1, source_target_pairs={{0,48},{24,72},{48,0},{72,24},{1,49},{25,73},{49,1},{73,25},{2,50}... | collective-permute-start | bytes 2371592 | tf_op jit(solution)/shard_map/ppermute | solution.py:126
  134.9 46.4 %collective-permute-start.8 = (f16[3088,128]{1,0:T(8,128)(2,1)}, f16[3088,128]{1,0:T(8,128)(2,1)}, u32[]{:S(2)}, u32[]{:S(2)}) collective-permute-start(f16[3088,128]{1,0:T(8,128)(2,1)} %get-tuple-element.18), channel_id=1, source_target_pairs={{0,72},{24,0},{48,24},{72,48},{1,73},{25,1},{49,25},{73,49},{2,74}... | collective-permute-start | bytes 2371592 | tf_op jit(solution)/shard_map/ppermute | solution.py:126
  187.4 9.7 %copy-start.2 = (bf16[24,128,128]{2,1,0:T(8,128)(2,1)S(1)}, bf16[24,128,128]{2,1,0:T(8,128)(2,1)}, u32[]{:S(2)}) copy-start(bf16[24,128,128]{2,1,0:T(8,128)(2,1)} %all-gather.3.refs_1_) | copy-start | bytes 2359300
  188.7 25.6 %all-to-all-start.3 = ((f16[24,144,128]{2,1,0:T(8,128)(2,1)}), f16[24,144,128]{2,1,0:T(8,128)(2,1)}, u32[]{:S(2)}, u32[]{:S(2)}) async-start(f16[24,144,128]{2,1,0:T(8,128)(2,1)} %select_convert_fusion), calls=%async_computation.3 | async-start | bytes 1769472 | tf_op jit(solution)/shard_map/all_to_all | solution.py:121
  197.1 34.1 %collective-permute-start.3 = (bf16[24,128,128]{2,1,0:T(8,128)(2,1)S(1)}, bf16[24,128,128]{2,1,0:T(8,128)(2,1)S(1)}, u32[]{:S(2)}, u32[]{:S(2)}) collective-permute-start(bf16[24,128,128]{2,1,0:T(8,128)(2,1)S(1)} %copy-done.2), channel_id=1, source_target_pairs={{0,24},{24,48},{48,72},{72,0},{1,25},{25,49},{49,73},{73,1},{2,26}... | collective-permute-start | bytes 2359304 | tf_op jit(solution)/shard_map/ppermute | solution.py:126
  199.4 31.9 %collective-permute-start.4 = (bf16[24,128,128]{2,1,0:T(8,128)(2,1)S(1)}, bf16[24,128,128]{2,1,0:T(8,128)(2,1)}, u32[]{:S(2)}, u32[]{:S(2)}) collective-permute-start(bf16[24,128,128]{2,1,0:T(8,128)(2,1)S(1)} %copy-done.2), channel_id=1, source_target_pairs={{0,48},{24,72},{48,0},{72,24},{1,49},{25,73},{49,1},{73,25},{2,50}... | collective-permute-start | bytes 2359304 | tf_op jit(solution)/shard_map/ppermute | solution.py:126
  202.5 32.0 %collective-permute-start.5 = (bf16[24,128,128]{2,1,0:T(8,128)(2,1)S(1)}, bf16[24,128,128]{2,1,0:T(8,128)(2,1)}, u32[]{:S(2)}, u32[]{:S(2)}) collective-permute-start(bf16[24,128,128]{2,1,0:T(8,128)(2,1)S(1)} %copy-done.2), channel_id=1, source_target_pairs={{0,72},{24,0},{48,24},{72,48},{1,73},{25,1},{49,25},{73,49},{2,74}... | collective-permute-start | bytes 2359304 | tf_op jit(solution)/shard_map/ppermute | solution.py:126
  217.9 19.0 %all-to-all-start.4 = ((f32[32,16,128]{2,1,0:T(8,128)}), f32[32,16,128]{2,1,0:T(8,128)S(1)}, u32[]{:S(2)}, u32[]{:S(2)}) async-start(f32[32,16,128]{2,1,0:T(8,128)} %bitcast.42), calls=%async_computation.4 | async-start | bytes 524288 | tf_op jit(solution)/shard_map/all_to_all | solution.py:121
  258.1 31.2 %all-to-all-start.2 = ((f32[8,128,128]{2,1,0:T(8,128)}), f32[8,128,128]{2,1,0:T(8,128)S(1)}, u32[]{:S(2)}, u32[]{:S(2)}) async-start(f32[8,128,128]{2,1,0:T(8,128)} %copy-done.5), calls=%async_computation.2 | async-start | bytes 1048576 | tf_op jit(solution)/shard_map/all_to_all | solution.py:121
  289.3 25.2 %all-to-all-start.6 = ((f32[32,16,128]{2,1,0:T(8,128)}), f32[32,16,128]{2,1,0:T(8,128)S(1)}, u32[]{:S(2)}, u32[]{:S(2)}) async-start(f32[32,16,128]{2,1,0:T(8,128)} %broadcast_in_dim.38), calls=%async_computation.6 | async-start | bytes 524288 | tf_op jit(solution)/shard_map/all_to_all | solution.py:121
  (5 other events, 5.4 us)

commit v4 on v3

--- a/solution.py
+++ b/solution.py
@@ -143,8 +143,8 @@
 
 
 def unpack(packed, base=14.0):
-    power = packed[..., -1:, :1].astype(jnp.float32)
-    return packed[..., :-16, :].astype(jnp.float32) / jnp.exp2(base - power), jnp.max(power)
+    power = packed[..., -1:, :].astype(jnp.float32)
+    return packed[..., :-16, :].astype(jnp.float32) / jnp.exp2(base - power), power
 
 
 def local(features, adj_blocks, positions, counts, w_in, w_out, cotangent):
@@ -192,10 +192,10 @@
     )
     class_rows = jnp.dot(hidden, w_out, preferred_element_type=jnp.float32).astype(jnp.bfloat16)
 
-    top = after(top, class_rows)
     bound = 0.01953125 * out_blocks * size
     most = jnp.clip(jnp.max(top), 1e-30, 1e38 / bound) * bound
-    power = jnp.ceil(jnp.log2(most)) + 1.0
+    power = jnp.broadcast_to(jnp.ceil(jnp.log2(most)) + 1.0, top.shape)
+    power = after(power, class_rows)[:1]
     flat = [part.reshape(-1, width) for part in partial_two]
     packed = lax.optimization_barrier([pack(part, power) for part in flat[1:]])
 
@@ -203,7 +203,7 @@
     groups_two = share_x(near_two.reshape(per_group, size, width))
     partial_out = forward(groups_two, "forward_two")
 
-    base = after(jnp.full(top.shape, 14.0, jnp.float32), near_two)[0, 0]
+    base = after(jnp.full(top.shape, 14.0, jnp.float32), near_two)[:1]
     total = flat[0]
     for d, part in enumerate(packed, 1):
         part, other = unpack(send_ahead(part, "x", d), base)

time: 317 us -> 307 us (0.968)
  waiting for transfers between devices: 77.5 us -> 71.3 us
  local copies, waits for them, and re-layouts: 16 us -> 11.7 us
  Pallas kernels: 10.3 us -> 14.6 us
  between operations: 6.44 us -> 2.32 us
    slice x5 -> x1, local copies, waits for them, and re-layouts: 5.6 us -> 0.82 us  [unpack(): power = packed[..., -1:, :].astype(jnp.float32)]
    all_to_all x5, starting transfers between devices: 47.1 us -> 42.4 us  [exchange(): return lax.all_to_all(values, axes, 0, 0)]
    all_to_all x5, waiting for transfers between devices: 65.3 us -> 60.9 us  [exchange(): return lax.all_to_all(values, axes, 0, 0)]
    pallas_call x3, Pallas kernels: 5.11 us -> 9.39 us  [tile_product(): pl.pallas_call(body, out_shape=outs, in_specs=[smem] * 3 + [pl.BlockSpec(...]
    unnamed x31 -> x28, local copies, waits for them, and re-layouts: 6.72 us -> 6.61 us
  transfers between devices with their start and end apart: 14 -> 14, of which waited for: 6 -> 6; matrix products, arithmetic and copies ran while one was open for 3% -> 2% of each run, Pallas kernels for 2% -> 3%
where the time goes in v4:
time: 307 us; the launch traced here: 305 us
  blocking collectives  115 us (37%)
  starting transfers between devices  75.4 us (25%)
  waiting for transfers between devices  71.3 us (23%)
  Pallas kernels  14.6 us (5%)
  other arithmetic  13.8 us (4%)
  local copies, waits for them, and re-layouts  11.7 us (4%)
    all_to_all x5, waiting for transfers between devices, exchange(): return lax.all_to_all(values, axes, 0, 0)  60.9 us
    all_to_all x2, blocking collectives, exchange(): return lax.all_to_all(values, axes, 0, 0)  53.2 us
    all_to_all x5, starting transfers between devices, exchange(): return lax.all_to_all(values, axes, 0, 0)  42.4 us
    ppermute x9, starting transfers between devices, send_ahead(): lax.ppermute(values, axes, [(i, (i + distance) % size) for i in range(siz...  33 us
    all_gather x1, blocking collectives, local(): lax.all_gather(lax.all_gather(class_rows, 'zl', axis=0), 'y', axis=0)  27 us
    all_gather x1, blocking collectives, local(): lax.all_gather(group_grad, 'zh', axis=0).reshape(out_blocks, size, -1)  24 us
    ppermute x9, waiting for transfers between devices, send_ahead(): lax.ppermute(values, axes, [(i, (i + distance) % size) for i in range(siz...  10.4 us
    pallas_call x3, Pallas kernels, tile_product(): pl.pallas_call(body, out_shape=outs, in_specs=[smem] * 3 + [pl.BlockSpec(...  9.39 us
  transfers between devices with their start and end apart: 14, of which 6 were waited for; matrix products, arithmetic and copies ran while one was open for 2% of the time, Pallas kernels for 3%

profile of v4, /device:TPU:72, one launch (start us, length us, event | category | flops | bytes accessed | tf_op | source)
XLA Modules:
  0.0 305.4 jit_solution(9022658724805641494)
XLA Ops:
  1.6 31.9 %all_to_all.35.earlier_ref.refs_2_ = bf16[24,128,128]{2,1,0:T(8,128)(2,1)S(1)} all-to-all(bf16[24,128,128]{2,1,0:T(8,128)(2,1)S(1)} %broadcast_in_dim.51), channel_id=1, replica_groups=mesh['zh'=4,'core'=2,'x'=4,'y'=8,'zl'=3] {'y','zl'}, dimensions={0} | all-to-all | bytes 1572864 | tf_op jit(solution)/shard_map/all_to_all | solution.py:121
  33.5 3.4 %collective-permute-start = (bf16[24,128,128]{2,1,0:T(8,128)(2,1)S(1)}, bf16[24,128,128]{2,1,0:T(8,128)(2,1)S(1)}, u32[]{:S(2)}, u32[]{:S(2)}) collective-permute-start(bf16[24,128,128]{2,1,0:T(8,128)(2,1)S(1)} %all_to_all.35.earlier_ref.refs_2_), channel_id=1, source_target_pairs={{0,24},{24,48},{48,72},{72,0},{1,25},{25,49},{49,73},{73,1},{2,26}... | collective-permute-start | bytes 2359304 | tf_op jit(solution)/shard_map/ppermute | solution.py:126
  36.9 4.6 %collective-permute-start.1 = (bf16[24,128,128]{2,1,0:T(8,128)(2,1)S(1)}, bf16[24,128,128]{2,1,0:T(8,128)(2,1)}, u32[]{:S(2)}, u32[]{:S(2)}) collective-permute-start(bf16[24,128,128]{2,1,0:T(8,128)(2,1)S(1)} %all_to_all.35.earlier_ref.refs_2_), channel_id=1, source_target_pairs={{0,48},{24,72},{48,0},{72,24},{1,49},{25,73},{49,1},{73,25},{2,50}... | collective-permute-start | bytes 2359304 | tf_op jit(solution)/shard_map/ppermute | solution.py:126
  41.5 3.3 %collective-permute-start.2 = (bf16[24,128,128]{2,1,0:T(8,128)(2,1)S(1)}, bf16[24,128,128]{2,1,0:T(8,128)(2,1)}, u32[]{:S(2)}, u32[]{:S(2)}) collective-permute-start(bf16[24,128,128]{2,1,0:T(8,128)(2,1)S(1)} %all_to_all.35.earlier_ref.refs_2_), channel_id=1, source_target_pairs={{0,72},{24,0},{48,24},{72,48},{1,73},{25,1},{49,25},{73,49},{2,74}... | collective-permute-start | bytes 2359304 | tf_op jit(solution)/shard_map/ppermute | solution.py:126
  49.1 24.0 %all-gather.1.refs_0_.refs_1_ = bf16[8,128,128]{2,1,0:T(8,128)(2,1)S(1)} all-gather(bf16[2,128,128]{2,1,0:T(8,128)(2,1)S(1)} %bitcast.51), channel_id=3, replica_groups=mesh['zh'=4,'core'=2,'x'=4,'y'=8,'zl'=3] {'zh'}, dimensions={0}, use_global_device_ids=true | all-gather | bytes 327680 | tf_op jit(solution)/shard_map/all_gather | solution.py:176
  74.2 3.6 %forward_one.1 = f32[8,128,128]{2,1,0:T(8,128)} custom-call(s32[1]{0:T(128)S(6)} %copy.14.count_ref, s32[1,48]{1,0:T(1,128)S(1)} %copy-done.11, s32[3]{0:T(128)S(1)} %pad_add_fusion.here_ref, bf16[8,128,128]{2,1,0:T(8,128)(2,1)S(1)} %all-gather.1.refs_0_.refs_1_, bf16[48,128,128]{2,1,0:T(8,128)(2,1)S(1)} %copy-done.1, bf16[24,128,128]{2,1,0:T(8,128)(2,1)S(1)} %copy-done.4, ...), custom_call_target="tpu_custom_call" | custom-call | flops 1 | bytes 1 | tf_op jit(solution)/shard_map/forward_one/pallas_call | solution.py:107
  77.8 13.7 %all-to-all-start.1 = ((f32[8,128,128]{2,1,0:T(8,128)}), f32[8,128,128]{2,1,0:T(8,128)S(1)}, u32[]{:S(2)}, u32[]{:S(2)}) async-start(f32[8,128,128]{2,1,0:T(8,128)} %forward_one.1), calls=%async_computation.1 | async-start | bytes 1048576 | tf_op jit(solution)/shard_map/all_to_all | solution.py:121
  100.4 16.9 %all-to-all-done.1 = f32[8,128,128]{2,1,0:T(8,128)S(1)} async-done(((f32[8,128,128]{2,1,0:T(8,128)}), f32[8,128,128]{2,1,0:T(8,128)S(1)}, u32[]{:S(2)}, u32[]{:S(2)}) %all-to-all-start.1) | async-done | bytes 524320 | tf_op jit(solution)/shard_map/all_to_all | solution.py:121
  120.8 4.3 %select_convert_fusion.1 = (f16[3088,128]{1,0:T(8,128)(2,1)}, f16[3088,128]{1,0:T(8,128)(2,1)}, f16[3088,128]{1,0:T(8,128)(2,1)}) fusion(f32[3072,128]{1,0:T(8,128)} %bitcast.47, f32[128]{0:T(128)S(1)} %get-tuple-element.32, f32[128]{0:T(128)S(1)} %get-tuple-element.31, pred[3088]{0:T(1024)(128)(4,1)S(1)} %iota_compare_fusion, f32[3072,128]{1,0:T(8,128)} %bitcast.46, ...), kind=kLoop, calls=%fused_computation.1 | loop fusion | flops 3557376 | bytes 7094288 | tf_op jit(solution)/shard_map/convert_element_type | solution.py:142
  128.1 5.1 %collective-permute-start.7 = (f16[3088,128]{1,0:T(8,128)(2,1)}, f16[3088,128]{1,0:T(8,128)(2,1)}, u32[]{:S(2)}, u32[]{:S(2)}) collective-permute-start(f16[3088,128]{1,0:T(8,128)(2,1)} %get-tuple-element.17), channel_id=1, source_target_pairs={{0,48},{24,72},{48,0},{72,24},{1,49},{25,73},{49,1},{73,25},{2,50}... | collective-permute-start | bytes 2371592 | tf_op jit(solution)/shard_map/ppermute | solution.py:126
  133.2 3.6 %collective-permute-start.8 = (f16[3088,128]{1,0:T(8,128)(2,1)}, f16[3088,128]{1,0:T(8,128)(2,1)}, u32[]{:S(2)}, u32[]{:S(2)}) collective-permute-start(f16[3088,128]{1,0:T(8,128)(2,1)} %get-tuple-element.18), channel_id=1, source_target_pairs={{0,72},{24,0},{48,24},{72,48},{1,73},{25,1},{49,25},{73,49},{2,74}... | collective-permute-start | bytes 2371592 | tf_op jit(solution)/shard_map/ppermute | solution.py:126
  136.8 8.6 %all-gather.2 = bf16[384,128]{1,0:T(8,128)(2,1)S(1)} all-gather(bf16[128,128]{1,0:T(8,128)(2,1)S(1)} %copy-done.12), channel_id=4, replica_groups=mesh['zh'=4,'core'=2,'x'=4,'y'=8,'zl'=3] {'zl'}, dimensions={0}, use_global_device_ids=true | all-gather | bytes 131072 | tf_op jit(solution)/shard_map/all_gather | solution.py:202
  145.5 27.0 %all-gather.3.refs_1_ = bf16[24,128,128]{2,1,0:T(8,128)(2,1)} all-gather(bf16[3,128,128]{2,1,0:T(8,128)(2,1)S(1)} %bitcast.50), channel_id=5, replica_groups=mesh['zh'=4,'core'=2,'x'=4,'y'=8,'zl'=3] {'y'}, dimensions={0}, use_global_device_ids=true | all-gather | bytes 884736 | tf_op jit(solution)/shard_map/all_gather | solution.py:202
  178.5 7.4 %all-to-all-start.3 = ((f16[24,144,128]{2,1,0:T(8,128)(2,1)}), f16[24,144,128]{2,1,0:T(8,128)(2,1)}, u32[]{:S(2)}, u32[]{:S(2)}) async-start(f16[24,144,128]{2,1,0:T(8,128)(2,1)} %select_convert_fusion), calls=%async_computation.3 | async-start | bytes 1769472 | tf_op jit(solution)/shard_map/all_to_all | solution.py:121
  189.0 3.4 %collective-permute-start.4 = (bf16[24,128,128]{2,1,0:T(8,128)(2,1)S(1)}, bf16[24,128,128]{2,1,0:T(8,128)(2,1)}, u32[]{:S(2)}, u32[]{:S(2)}) collective-permute-start(bf16[24,128,128]{2,1,0:T(8,128)(2,1)S(1)} %copy-done.2), channel_id=1, source_target_pairs={{0,48},{24,72},{48,0},{72,24},{1,49},{25,73},{49,1},{73,25},{2,50}... | collective-permute-start | bytes 2359304 | tf_op jit(solution)/shard_map/ppermute | solution.py:126
  192.4 3.4 %collective-permute-start.5 = (bf16[24,128,128]{2,1,0:T(8,128)(2,1)S(1)}, bf16[24,128,128]{2,1,0:T(8,128)(2,1)}, u32[]{:S(2)}, u32[]{:S(2)}) collective-permute-start(bf16[24,128,128]{2,1,0:T(8,128)(2,1)S(1)} %copy-done.2), channel_id=1, source_target_pairs={{0,72},{24,0},{48,24},{72,48},{1,73},{25,1},{49,25},{73,49},{2,74}... | collective-permute-start | bytes 2359304 | tf_op jit(solution)/shard_map/ppermute | solution.py:126
  195.8 7.5 %all-to-all-done.3 = f16[24,144,128]{2,1,0:T(8,128)(2,1)} async-done(((f16[24,144,128]{2,1,0:T(8,128)(2,1)}), f16[24,144,128]{2,1,0:T(8,128)(2,1)}, u32[]{:S(2)}, u32[]{:S(2)}) %all-to-all-start.3) | async-done | bytes 884768 | tf_op jit(solution)/shard_map/all_to_all | solution.py:121
  206.7 6.6 %all-to-all-start.4 = ((f32[32,16,128]{2,1,0:T(8,128)}), f32[32,16,128]{2,1,0:T(8,128)S(1)}, u32[]{:S(2)}, u32[]{:S(2)}) async-start(f32[32,16,128]{2,1,0:T(8,128)} %bitcast.49), calls=%async_computation.4 | async-start | bytes 524288 | tf_op jit(solution)/shard_map/all_to_all | solution.py:121
  213.4 8.4 %collective-permute-done.4.refs_3_ = bf16[24,128,128]{2,1,0:T(8,128)(2,1)} collective-permute-done((bf16[24,128,128]{2,1,0:T(8,128)(2,1)S(1)}, bf16[24,128,128]{2,1,0:T(8,128)(2,1)}, u32[]{:S(2)}, u32[]{:S(2)}) %collective-permute-start.4) | collective-permute-done | bytes 786464 | tf_op jit(solution)/shard_map/ppermute | solution.py:126
  230.0 21.4 %all_to_all.36 = f32[24,16,128]{2,1,0:T(8,128)S(1)} all-to-all(f32[24,16,128]{2,1,0:T(8,128)S(1)} %broadcast_in_dim.57), channel_id=1, replica_groups=mesh['zh'=4,'core'=2,'x'=4,'y'=8,'zl'=3] {'zh','core','zl'}, dimensions={0} | all-to-all | bytes 393216 | tf_op jit(solution)/shard_map/all_to_all | solution.py:121
  251.4 5.5 %all-to-all-start.2 = ((f32[8,128,128]{2,1,0:T(8,128)}), f32[8,128,128]{2,1,0:T(8,128)S(1)}, u32[]{:S(2)}, u32[]{:S(2)}) async-start(f32[8,128,128]{2,1,0:T(8,128)} %copy-done.5), calls=%async_computation.2 | async-start | bytes 1048576 | tf_op jit(solution)/shard_map/all_to_all | solution.py:121
  257.6 25.0 %all-to-all-done.2 = f32[8,128,128]{2,1,0:T(8,128)S(1)} async-done(((f32[8,128,128]{2,1,0:T(8,128)}), f32[8,128,128]{2,1,0:T(8,128)S(1)}, u32[]{:S(2)}, u32[]{:S(2)}) %all-to-all-start.2) | async-done | bytes 524320 | tf_op jit(solution)/shard_map/all_to_all | solution.py:121
  282.6 9.2 %all-to-all-start.6 = ((f32[32,16,128]{2,1,0:T(8,128)}), f32[32,16,128]{2,1,0:T(8,128)S(1)}, u32[]{:S(2)}, u32[]{:S(2)}) async-start(f32[32,16,128]{2,1,0:T(8,128)} %broadcast_in_dim.58), calls=%async_computation.6 | async-start | bytes 524288 | tf_op jit(solution)/shard_map/all_to_all | solution.py:121
  292.5 11.6 %all-to-all-done.6 = f32[32,16,128]{2,1,0:T(8,128)S(1)} async-done(((f32[32,16,128]{2,1,0:T(8,128)}), f32[32,16,128]{2,1,0:T(8,128)S(1)}, u32[]{:S(2)}, u32[]{:S(2)}) %all-to-all-start.6) | async-done | bytes 262176 | tf_op jit(solution)/shard_map/all_to_all | solution.py:121
  (75 shorter events, 43.6 us)
Async XLA Ops:
  0.6 116.8 %copy-start = (bf16[256,128]{1,0:T(8,128)(2,1)S(1)}, bf16[256,128]{1,0:T(8,128)(2,1)}, u32[]{:S(2)}) copy-start(bf16[256,128]{1,0:T(8,128)(2,1)} %param.12) | copy-start | bytes 196612
  1.6 71.4 %copy-start.1 = (bf16[48,128,128]{2,1,0:T(8,128)(2,1)S(1)}, bf16[48,128,128]{2,1,0:T(8,128)(2,1)}, u32[]{:S(2)}) copy-start(bf16[48,128,128]{2,1,0:T(8,128)(2,1)} %refs_0_.3) | copy-start | bytes 4718596
  1.6 71.4 %copy-start.11 = (s32[1,48]{1,0:T(1,128)S(1)}, s32[1,48]{1,0:T(1,128)}, u32[]{:S(2)}) copy-start(s32[1,48]{1,0:T(1,128)} %place_ref.5) | copy-start | bytes 580
  33.5 12.1 %copy-start.3 = (bf16[24,128,128]{2,1,0:T(8,128)(2,1)}, bf16[24,128,128]{2,1,0:T(8,128)(2,1)S(1)}, u32[]{:S(2)}) copy-start(bf16[24,128,128]{2,1,0:T(8,128)(2,1)S(1)} %all_to_all.35.earlier_ref.refs_2_) | copy-start | bytes 2359300
  33.5 39.5 %collective-permute-start = (bf16[24,128,128]{2,1,0:T(8,128)(2,1)S(1)}, bf16[24,128,128]{2,1,0:T(8,128)(2,1)S(1)}, u32[]{:S(2)}, u32[]{:S(2)}) collective-permute-start(bf16[24,128,128]{2,1,0:T(8,128)(2,1)S(1)} %all_to_all.35.earlier_ref.refs_2_), channel_id=1, source_target_pairs={{0,24},{24,48},{48,72},{72,0},{1,25},{25,49},{49,73},{73,1},{2,26}... | collective-permute-start | bytes 2359304 | tf_op jit(solution)/shard_map/ppermute | solution.py:126
  36.9 36.1 %collective-permute-start.1 = (bf16[24,128,128]{2,1,0:T(8,128)(2,1)S(1)}, bf16[24,128,128]{2,1,0:T(8,128)(2,1)}, u32[]{:S(2)}, u32[]{:S(2)}) collective-permute-start(bf16[24,128,128]{2,1,0:T(8,128)(2,1)S(1)} %all_to_all.35.earlier_ref.refs_2_), channel_id=1, source_target_pairs={{0,48},{24,72},{48,0},{72,24},{1,49},{25,73},{49,1},{73,25},{2,50}... | collective-permute-start | bytes 2359304 | tf_op jit(solution)/shard_map/ppermute | solution.py:126
  41.5 31.5 %collective-permute-start.2 = (bf16[24,128,128]{2,1,0:T(8,128)(2,1)S(1)}, bf16[24,128,128]{2,1,0:T(8,128)(2,1)}, u32[]{:S(2)}, u32[]{:S(2)}) collective-permute-start(bf16[24,128,128]{2,1,0:T(8,128)(2,1)S(1)} %all_to_all.35.earlier_ref.refs_2_), channel_id=1, source_target_pairs={{0,72},{24,0},{48,24},{72,48},{1,73},{25,1},{49,25},{73,49},{2,74}... | collective-permute-start | bytes 2359304 | tf_op jit(solution)/shard_map/ppermute | solution.py:126
  77.8 39.5 %copy-start.13 = (bf16[128,256]{1,0:T(8,128)(2,1)S(1)}, bf16[128,256]{1,0:T(8,128)(2,1)}, u32[]{:S(2)}) copy-start(bf16[128,256]{1,0:T(8,128)(2,1)} %param.11) | copy-start | bytes 196612
  77.8 39.4 %all-to-all-start.1 = ((f32[8,128,128]{2,1,0:T(8,128)}), f32[8,128,128]{2,1,0:T(8,128)S(1)}, u32[]{:S(2)}, u32[]{:S(2)}) async-start(f32[8,128,128]{2,1,0:T(8,128)} %forward_one.1), calls=%async_computation.1 | async-start | bytes 1048576 | tf_op jit(solution)/shard_map/all_to_all | solution.py:121
  94.4 1.2 copy-start.6
  95.6 1.2 copy-start.8
  120.8 16.0 %copy-start.12 = (bf16[128,128]{1,0:T(8,128)(2,1)S(1)}, bf16[128,128]{1,0:T(8,128)(2,1)}, u32[]{:S(2)}) copy-start(bf16[128,128]{1,0:T(8,128)(2,1)} %convolution_convert_fusion.earlier_ref) | copy-start | bytes 98308
  125.0 50.1 %copy-start.7 = (f32[24,128,128]{2,1,0:T(8,128)S(1)}, f32[24,128,128]{2,1,0:T(8,128)}, u32[]{:S(2)}) copy-start(f32[24,128,128]{2,1,0:T(8,128)} %copy-done.6) | copy-start | bytes 4718596
  125.0 49.3 %collective-permute-start.6 = (f16[3088,128]{1,0:T(8,128)(2,1)}, f16[3088,128]{1,0:T(8,128)(2,1)}, u32[]{:S(2)}, u32[]{:S(2)}) collective-permute-start(f16[3088,128]{1,0:T(8,128)(2,1)} %get-tuple-element.16), channel_id=1, source_target_pairs={{0,24},{24,48},{48,72},{72,0},{1,25},{25,49},{49,73},{73,1},{2,26}... | collective-permute-start | bytes 2371592 | tf_op jit(solution)/shard_map/ppermute | solution.py:126
  128.1 46.3 %collective-permute-start.7 = (f16[3088,128]{1,0:T(8,128)(2,1)}, f16[3088,128]{1,0:T(8,128)(2,1)}, u32[]{:S(2)}, u32[]{:S(2)}) collective-permute-start(f16[3088,128]{1,0:T(8,128)(2,1)} %get-tuple-element.17), channel_id=1, source_target_pairs={{0,48},{24,72},{48,0},{72,24},{1,49},{25,73},{49,1},{73,25},{2,50}... | collective-permute-start | bytes 2371592 | tf_op jit(solution)/shard_map/ppermute | solution.py:126
  133.2 41.2 %collective-permute-start.8 = (f16[3088,128]{1,0:T(8,128)(2,1)}, f16[3088,128]{1,0:T(8,128)(2,1)}, u32[]{:S(2)}, u32[]{:S(2)}) collective-permute-start(f16[3088,128]{1,0:T(8,128)(2,1)} %get-tuple-element.18), channel_id=1, source_target_pairs={{0,72},{24,0},{48,24},{72,48},{1,73},{25,1},{49,25},{73,49},{2,74}... | collective-permute-start | bytes 2371592 | tf_op jit(solution)/shard_map/ppermute | solution.py:126
  177.3 8.7 %copy-start.2 = (bf16[24,128,128]{2,1,0:T(8,128)(2,1)S(1)}, bf16[24,128,128]{2,1,0:T(8,128)(2,1)}, u32[]{:S(2)}) copy-start(bf16[24,128,128]{2,1,0:T(8,128)(2,1)} %all-gather.3.refs_1_) | copy-start | bytes 2359300
  178.5 24.8 %all-to-all-start.3 = ((f16[24,144,128]{2,1,0:T(8,128)(2,1)}), f16[24,144,128]{2,1,0:T(8,128)(2,1)}, u32[]{:S(2)}, u32[]{:S(2)}) async-start(f16[24,144,128]{2,1,0:T(8,128)(2,1)} %select_convert_fusion), calls=%async_computation.3 | async-start | bytes 1769472 | tf_op jit(solution)/shard_map/all_to_all | solution.py:121
  186.0 27.4 %collective-permute-start.3 = (bf16[24,128,128]{2,1,0:T(8,128)(2,1)S(1)}, bf16[24,128,128]{2,1,0:T(8,128)(2,1)S(1)}, u32[]{:S(2)}, u32[]{:S(2)}) collective-permute-start(bf16[24,128,128]{2,1,0:T(8,128)(2,1)S(1)} %copy-done.2), channel_id=1, source_target_pairs={{0,24},{24,48},{48,72},{72,0},{1,25},{25,49},{49,73},{73,1},{2,26}... | collective-permute-start | bytes 2359304 | tf_op jit(solution)/shard_map/ppermute | solution.py:126
  189.0 32.8 %collective-permute-start.4 = (bf16[24,128,128]{2,1,0:T(8,128)(2,1)S(1)}, bf16[24,128,128]{2,1,0:T(8,128)(2,1)}, u32[]{:S(2)}, u32[]{:S(2)}) collective-permute-start(bf16[24,128,128]{2,1,0:T(8,128)(2,1)S(1)} %copy-done.2), channel_id=1, source_target_pairs={{0,48},{24,72},{48,0},{72,24},{1,49},{25,73},{49,1},{73,25},{2,50}... | collective-permute-start | bytes 2359304 | tf_op jit(solution)/shard_map/ppermute | solution.py:126
  192.4 31.3 %collective-permute-start.5 = (bf16[24,128,128]{2,1,0:T(8,128)(2,1)S(1)}, bf16[24,128,128]{2,1,0:T(8,128)(2,1)}, u32[]{:S(2)}, u32[]{:S(2)}) collective-permute-start(bf16[24,128,128]{2,1,0:T(8,128)(2,1)S(1)} %copy-done.2), channel_id=1, source_target_pairs={{0,72},{24,0},{48,24},{72,48},{1,73},{25,1},{49,25},{73,49},{2,74}... | collective-permute-start | bytes 2359304 | tf_op jit(solution)/shard_map/ppermute | solution.py:126
  206.7 20.6 %all-to-all-start.4 = ((f32[32,16,128]{2,1,0:T(8,128)}), f32[32,16,128]{2,1,0:T(8,128)S(1)}, u32[]{:S(2)}, u32[]{:S(2)}) async-start(f32[32,16,128]{2,1,0:T(8,128)} %bitcast.49), calls=%async_computation.4 | async-start | bytes 524288 | tf_op jit(solution)/shard_map/all_to_all | solution.py:121
  251.4 31.2 %all-to-all-start.2 = ((f32[8,128,128]{2,1,0:T(8,128)}), f32[8,128,128]{2,1,0:T(8,128)S(1)}, u32[]{:S(2)}, u32[]{:S(2)}) async-start(f32[8,128,128]{2,1,0:T(8,128)} %copy-done.5), calls=%async_computation.2 | async-start | bytes 1048576 | tf_op jit(solution)/shard_map/all_to_all | solution.py:121
  282.6 21.5 %all-to-all-start.6 = ((f32[32,16,128]{2,1,0:T(8,128)}), f32[32,16,128]{2,1,0:T(8,128)S(1)}, u32[]{:S(2)}, u32[]{:S(2)}) async-start(f32[32,16,128]{2,1,0:T(8,128)} %broadcast_in_dim.58), calls=%async_computation.6 | async-start | bytes 524288 | tf_op jit(solution)/shard_map/all_to_all | solution.py:121
  (4 other events, 4.2 us)

commit v5 on v4

--- a/solution.py
+++ b/solution.py
@@ -222,8 +222,11 @@
     parts = [local_in[:, i * classes : (i + 1) * classes] for i in range(halves)]
     grads = jnp.concatenate(parts + [local_out], axis=0).reshape(planes, -1, classes)
     grads = jnp.sum(exchange(grads, ("x", "y")), axis=0)
-    output = jnp.sum(exchange(partial_out, ROW), axis=0).astype(jnp.bfloat16)
-    grads = jnp.sum(share(after(grads, partial_out), ("zh", "core", "zl")), axis=0)
+    copies = jnp.broadcast_to(grads[None], (lax.axis_size(ROW),) + grads.shape)
+    last = exchange(jnp.concatenate([partial_out, copies], axis=1), ROW)
+    last = jnp.sum(last, axis=0)
+    output = last[:size].astype(jnp.bfloat16)
+    grads = jnp.sum(lax.all_gather(last[size:], "zl", axis=0), axis=0)
     grads = share(grads, ("x", "y")).reshape(-1, classes)
     rows_in = local_in.shape[0]
     grad_in = jnp.concatenate(

time: 307 us -> 297 us (0.967)
  the two profiles are of different devices: /device:TPU:72 before, /device:TPU:1 now
where the time goes in v5:
time: 297 us; the launch traced here: 293 us
  blocking collectives  140 us (47%)
  starting transfers between devices  74.5 us (25%)
  waiting for transfers between devices  34.6 us (12%)
  local copies, waits for them, and re-layouts  13.4 us (5%)
  Pallas kernels  12.9 us (4%)
  other arithmetic  12.5 us (4%)
    all_to_all x2, blocking collectives, exchange(): return lax.all_to_all(values, axes, 0, 0)  61.6 us
    all_to_all x4, starting transfers between devices, exchange(): return lax.all_to_all(values, axes, 0, 0)  43.1 us
    ppermute x9, starting transfers between devices, send_ahead(): lax.ppermute(values, axes, [(i, (i + distance) % size) for i in range(siz...  31.4 us
    all_gather x1, blocking collectives, local(): lax.all_gather(lax.all_gather(class_rows, 'zl', axis=0), 'y', axis=0)  25.8 us
    all_to_all x4, waiting for transfers between devices, exchange(): return lax.all_to_all(values, axes, 0, 0)  25.3 us
    all_gather x1, blocking collectives, local(): lax.all_gather(group_grad, 'zh', axis=0).reshape(out_blocks, size, -1)  21.2 us
    all_gather x1, blocking collectives, local(): lax.all_gather(class_rows, 'zl', axis=0)  17.2 us
    ppermute x9, waiting for transfers between devices, send_ahead(): lax.ppermute(values, axes, [(i, (i + distance) % size) for i in range(siz...  9.32 us
  transfers between devices with their start and end apart: 13, of which 4 were waited for; matrix products, arithmetic and copies ran while one was open for 2% of the time, Pallas kernels for 3%

profile of v5, /device:TPU:1, one launch (start us, length us, event | category | flops | bytes accessed | tf_op | source)
XLA Modules:
  0.0 292.9 jit_solution(2273196283665343475)
XLA Ops:
  1.6 28.8 %all_to_all.30.earlier_ref.refs_2_ = bf16[24,128,128]{2,1,0:T(8,128)(2,1)S(1)} all-to-all(bf16[24,128,128]{2,1,0:T(8,128)(2,1)S(1)} %broadcast_in_dim.51), channel_id=1, replica_groups=mesh['zh'=4,'core'=2,'x'=4,'y'=8,'zl'=3] {'y','zl'}, dimensions={0} | all-to-all | bytes 1572864 | tf_op jit(solution)/shard_map/all_to_all | solution.py:121
  30.4 4.1 %collective-permute-start = (bf16[24,128,128]{2,1,0:T(8,128)(2,1)S(1)}, bf16[24,128,128]{2,1,0:T(8,128)(2,1)S(1)}, u32[]{:S(2)}, u32[]{:S(2)}) collective-permute-start(bf16[24,128,128]{2,1,0:T(8,128)(2,1)S(1)} %all_to_all.30.earlier_ref.refs_2_), channel_id=1, source_target_pairs={{0,24},{24,48},{48,72},{72,0},{1,25},{25,49},{49,73},{73,1},{2,26}... | collective-permute-start | bytes 2359304 | tf_op jit(solution)/shard_map/ppermute | solution.py:126
  34.5 4.4 %collective-permute-start.1 = (bf16[24,128,128]{2,1,0:T(8,128)(2,1)S(1)}, bf16[24,128,128]{2,1,0:T(8,128)(2,1)}, u32[]{:S(2)}, u32[]{:S(2)}) collective-permute-start(bf16[24,128,128]{2,1,0:T(8,128)(2,1)S(1)} %all_to_all.30.earlier_ref.refs_2_), channel_id=1, source_target_pairs={{0,48},{24,72},{48,0},{72,24},{1,49},{25,73},{49,1},{73,25},{2,50}... | collective-permute-start | bytes 2359304 | tf_op jit(solution)/shard_map/ppermute | solution.py:126
  38.9 3.1 %collective-permute-start.2 = (bf16[24,128,128]{2,1,0:T(8,128)(2,1)S(1)}, bf16[24,128,128]{2,1,0:T(8,128)(2,1)}, u32[]{:S(2)}, u32[]{:S(2)}) collective-permute-start(bf16[24,128,128]{2,1,0:T(8,128)(2,1)S(1)} %all_to_all.30.earlier_ref.refs_2_), channel_id=1, source_target_pairs={{0,72},{24,0},{48,24},{72,48},{1,73},{25,1},{49,25},{73,49},{2,74}... | collective-permute-start | bytes 2359304 | tf_op jit(solution)/shard_map/ppermute | solution.py:126
  44.1 7.5 %all-gather = bf16[256,128]{1,0:T(8,128)(2,1)S(1)} all-gather(bf16[128,128]{1,0:T(8,128)(2,1)} %after.3), channel_id=2, replica_groups=mesh['zh'=4,'core'=2,'x'=4,'y'=8,'zl'=3] {'core'}, dimensions={0}, use_global_device_ids=true | all-gather | bytes 98304 | tf_op jit(solution)/shard_map/all_gather | solution.py:175
  51.6 21.2 %all-gather.1.refs_0_.refs_1_ = bf16[8,128,128]{2,1,0:T(8,128)(2,1)S(1)} all-gather(bf16[2,128,128]{2,1,0:T(8,128)(2,1)S(1)} %bitcast.52), channel_id=3, replica_groups=mesh['zh'=4,'core'=2,'x'=4,'y'=8,'zl'=3] {'zh'}, dimensions={0}, use_global_device_ids=true | all-gather | bytes 327680 | tf_op jit(solution)/shard_map/all_gather | solution.py:176
  74.0 3.5 %forward_one.1 = f32[8,128,128]{2,1,0:T(8,128)} custom-call(s32[1]{0:T(128)S(6)} %copy.14.count_ref, s32[1,48]{1,0:T(1,128)S(1)} %copy-done.12, s32[3]{0:T(128)S(1)} %pad_add_fusion.here_ref, bf16[8,128,128]{2,1,0:T(8,128)(2,1)S(1)} %all-gather.1.refs_0_.refs_1_, bf16[48,128,128]{2,1,0:T(8,128)(2,1)S(1)} %copy-done.1, bf16[24,128,128]{2,1,0:T(8,128)(2,1)S(1)} %copy-done.4, ...), custom_call_target="tpu_custom_call" | custom-call | flops 1 | bytes 1 | tf_op jit(solution)/shard_map/forward_one/pallas_call | solution.py:107
  77.5 15.4 %all-to-all-start.1 = ((f32[8,128,128]{2,1,0:T(8,128)}), f32[8,128,128]{2,1,0:T(8,128)S(1)}, u32[]{:S(2)}, u32[]{:S(2)}) async-start(f32[8,128,128]{2,1,0:T(8,128)} %forward_one.1), calls=%async_computation.1 | async-start | bytes 1048576 | tf_op jit(solution)/shard_map/all_to_all | solution.py:121
  93.0 2.8 backward.1
  101.7 5.9 %all-to-all-done.1 = f32[8,128,128]{2,1,0:T(8,128)S(1)} async-done(((f32[8,128,128]{2,1,0:T(8,128)}), f32[8,128,128]{2,1,0:T(8,128)S(1)}, u32[]{:S(2)}, u32[]{:S(2)}) %all-to-all-start.1) | async-done | bytes 524320 | tf_op jit(solution)/shard_map/all_to_all | solution.py:121
  111.1 4.2 %select_convert_fusion.1 = (f16[3088,128]{1,0:T(8,128)(2,1)}, f16[3088,128]{1,0:T(8,128)(2,1)}, f16[3088,128]{1,0:T(8,128)(2,1)}) fusion(f32[3072,128]{1,0:T(8,128)} %bitcast.48, f32[128]{0:T(128)S(1)} %get-tuple-element.32, f32[128]{0:T(128)S(1)} %get-tuple-element.31, pred[3088]{0:T(1024)(128)(4,1)S(1)} %iota_compare_fusion, f32[3072,128]{1,0:T(8,128)} %bitcast.47, ...), kind=kLoop, calls=%fused_computation.1 | loop fusion | flops 3557376 | bytes 7094288 | tf_op jit(solution)/shard_map/convert_element_type | solution.py:142
  115.3 6.3 %collective-permute-start.8 = (f16[3088,128]{1,0:T(8,128)(2,1)}, f16[3088,128]{1,0:T(8,128)(2,1)}, u32[]{:S(2)}, u32[]{:S(2)}) collective-permute-start(f16[3088,128]{1,0:T(8,128)(2,1)} %get-tuple-element.18), channel_id=1, source_target_pairs={{0,72},{24,0},{48,24},{72,48},{1,73},{25,1},{49,25},{73,49},{2,74}... | collective-permute-start | bytes 2371592 | tf_op jit(solution)/shard_map/ppermute | solution.py:126
  126.0 17.2 %all-gather.2 = bf16[384,128]{1,0:T(8,128)(2,1)S(1)} all-gather(bf16[128,128]{1,0:T(8,128)(2,1)S(1)} %copy-done.15), channel_id=4, replica_groups=mesh['zh'=4,'core'=2,'x'=4,'y'=8,'zl'=3] {'zl'}, dimensions={0}, use_global_device_ids=true | all-gather | bytes 131072 | tf_op jit(solution)/shard_map/all_gather | solution.py:202
  143.3 25.8 %all-gather.3.refs_1_ = bf16[24,128,128]{2,1,0:T(8,128)(2,1)} all-gather(bf16[3,128,128]{2,1,0:T(8,128)(2,1)S(1)} %bitcast.51), channel_id=5, replica_groups=mesh['zh'=4,'core'=2,'x'=4,'y'=8,'zl'=3] {'y'}, dimensions={0}, use_global_device_ids=true | all-gather | bytes 884736 | tf_op jit(solution)/shard_map/all_gather | solution.py:202
  175.0 8.6 %all-to-all-start.2 = ((f16[24,144,128]{2,1,0:T(8,128)(2,1)}), f16[24,144,128]{2,1,0:T(8,128)(2,1)}, u32[]{:S(2)}, u32[]{:S(2)}) async-start(f16[24,144,128]{2,1,0:T(8,128)(2,1)} %select_convert_fusion), calls=%async_computation.2 | async-start | bytes 1769472 | tf_op jit(solution)/shard_map/all_to_all | solution.py:121
  185.6 3.4 %collective-permute-start.4 = (bf16[24,128,128]{2,1,0:T(8,128)(2,1)S(1)}, bf16[24,128,128]{2,1,0:T(8,128)(2,1)}, u32[]{:S(2)}, u32[]{:S(2)}) collective-permute-start(bf16[24,128,128]{2,1,0:T(8,128)(2,1)S(1)} %copy-done.2), channel_id=1, source_target_pairs={{0,48},{24,72},{48,0},{72,24},{1,49},{25,73},{49,1},{73,25},{2,50}... | collective-permute-start | bytes 2359304 | tf_op jit(solution)/shard_map/ppermute | solution.py:126
  189.0 4.0 %collective-permute-start.5 = (bf16[24,128,128]{2,1,0:T(8,128)(2,1)S(1)}, bf16[24,128,128]{2,1,0:T(8,128)(2,1)}, u32[]{:S(2)}, u32[]{:S(2)}) collective-permute-start(bf16[24,128,128]{2,1,0:T(8,128)(2,1)S(1)} %copy-done.2), channel_id=1, source_target_pairs={{0,72},{24,0},{48,24},{72,48},{1,73},{25,1},{49,25},{73,49},{2,74}... | collective-permute-start | bytes 2359304 | tf_op jit(solution)/shard_map/ppermute | solution.py:126
  193.0 10.3 %all-to-all-done.2 = f16[24,144,128]{2,1,0:T(8,128)(2,1)} async-done(((f16[24,144,128]{2,1,0:T(8,128)(2,1)}), f16[24,144,128]{2,1,0:T(8,128)(2,1)}, u32[]{:S(2)}, u32[]{:S(2)}) %all-to-all-start.2) | async-done | bytes 884768 | tf_op jit(solution)/shard_map/all_to_all | solution.py:121
  208.1 8.6 %all-to-all-start.3 = ((f32[32,16,128]{2,1,0:T(8,128)}), f32[32,16,128]{2,1,0:T(8,128)S(1)}, u32[]{:S(2)}, u32[]{:S(2)}) async-start(f32[32,16,128]{2,1,0:T(8,128)} %bitcast.50), calls=%async_computation.3 | async-start | bytes 524288 | tf_op jit(solution)/shard_map/all_to_all | solution.py:121
  217.6 9.3 %collective-permute-done.5.refs_4_ = bf16[24,128,128]{2,1,0:T(8,128)(2,1)} collective-permute-done((bf16[24,128,128]{2,1,0:T(8,128)(2,1)S(1)}, bf16[24,128,128]{2,1,0:T(8,128)(2,1)}, u32[]{:S(2)}, u32[]{:S(2)}) %collective-permute-start.5) | collective-permute-done | bytes 786464 | tf_op jit(solution)/shard_map/ppermute | solution.py:126
  230.8 32.8 %all_to_all.31 = f32[8,144,128]{2,1,0:T(8,128)S(1)} all-to-all(f32[8,144,128]{2,1,0:T(8,128)S(1)} %pad_maximum_fusion), channel_id=1, replica_groups=mesh['zh'=4,'core'=2,'x'=4,'y'=8,'zl'=3] {'zh','core'}, dimensions={0} | all-to-all | bytes 1179648 | tf_op jit(solution)/shard_map/all_to_all | solution.py:121
  263.7 7.0 %all-gather.4 = f32[48,128]{1,0:T(8,128)S(1)} all-gather(f32[16,128]{1,0:T(8,128)S(1)} %slice.92), channel_id=6, replica_groups=mesh['zh'=4,'core'=2,'x'=4,'y'=8,'zl'=3] {'zl'}, dimensions={0}, use_global_device_ids=true | all-gather | bytes 32768 | tf_op jit(solution)/shard_map/all_gather | solution.py:229
  271.3 10.4 %all-to-all-start.5 = ((f32[32,16,128]{2,1,0:T(8,128)}), f32[32,16,128]{2,1,0:T(8,128)S(1)}, u32[]{:S(2)}, u32[]{:S(2)}) async-start(f32[32,16,128]{2,1,0:T(8,128)} %broadcast_in_dim.58), calls=%async_computation.5 | async-start | bytes 524288 | tf_op jit(solution)/shard_map/all_to_all | solution.py:121
  282.4 9.1 %all-to-all-done.5 = f32[32,16,128]{2,1,0:T(8,128)S(1)} async-done(((f32[32,16,128]{2,1,0:T(8,128)}), f32[32,16,128]{2,1,0:T(8,128)S(1)}, u32[]{:S(2)}, u32[]{:S(2)}) %all-to-all-start.5) | async-done | bytes 262176 | tf_op jit(solution)/shard_map/all_to_all | solution.py:121
  (82 shorter events, 36.9 us)
Async XLA Ops:
  0.6 107.1 %copy-start = (bf16[256,128]{1,0:T(8,128)(2,1)S(1)}, bf16[256,128]{1,0:T(8,128)(2,1)}, u32[]{:S(2)}) copy-start(bf16[256,128]{1,0:T(8,128)(2,1)} %param.12) | copy-start | bytes 196612
  1.6 71.3 %copy-start.1 = (bf16[48,128,128]{2,1,0:T(8,128)(2,1)S(1)}, bf16[48,128,128]{2,1,0:T(8,128)(2,1)}, u32[]{:S(2)}) copy-start(bf16[48,128,128]{2,1,0:T(8,128)(2,1)} %refs_0_.3) | copy-start | bytes 4718596
  1.6 71.3 %copy-start.12 = (s32[1,48]{1,0:T(1,128)S(1)}, s32[1,48]{1,0:T(1,128)}, u32[]{:S(2)}) copy-start(s32[1,48]{1,0:T(1,128)} %place_ref.5) | copy-start | bytes 580
  30.4 12.2 %copy-start.3 = (bf16[24,128,128]{2,1,0:T(8,128)(2,1)}, bf16[24,128,128]{2,1,0:T(8,128)(2,1)S(1)}, u32[]{:S(2)}) copy-start(bf16[24,128,128]{2,1,0:T(8,128)(2,1)S(1)} %all_to_all.30.earlier_ref.refs_2_) | copy-start | bytes 2359300
  30.4 42.4 %collective-permute-start = (bf16[24,128,128]{2,1,0:T(8,128)(2,1)S(1)}, bf16[24,128,128]{2,1,0:T(8,128)(2,1)S(1)}, u32[]{:S(2)}, u32[]{:S(2)}) collective-permute-start(bf16[24,128,128]{2,1,0:T(8,128)(2,1)S(1)} %all_to_all.30.earlier_ref.refs_2_), channel_id=1, source_target_pairs={{0,24},{24,48},{48,72},{72,0},{1,25},{25,49},{49,73},{73,1},{2,26}... | collective-permute-start | bytes 2359304 | tf_op jit(solution)/shard_map/ppermute | solution.py:126
  34.5 38.3 %collective-permute-start.1 = (bf16[24,128,128]{2,1,0:T(8,128)(2,1)S(1)}, bf16[24,128,128]{2,1,0:T(8,128)(2,1)}, u32[]{:S(2)}, u32[]{:S(2)}) collective-permute-start(bf16[24,128,128]{2,1,0:T(8,128)(2,1)S(1)} %all_to_all.30.earlier_ref.refs_2_), channel_id=1, source_target_pairs={{0,48},{24,72},{48,0},{72,24},{1,49},{25,73},{49,1},{73,25},{2,50}... | collective-permute-start | bytes 2359304 | tf_op jit(solution)/shard_map/ppermute | solution.py:126
  38.9 34.0 %collective-permute-start.2 = (bf16[24,128,128]{2,1,0:T(8,128)(2,1)S(1)}, bf16[24,128,128]{2,1,0:T(8,128)(2,1)}, u32[]{:S(2)}, u32[]{:S(2)}) collective-permute-start(bf16[24,128,128]{2,1,0:T(8,128)(2,1)S(1)} %all_to_all.30.earlier_ref.refs_2_), channel_id=1, source_target_pairs={{0,72},{24,0},{48,24},{72,48},{1,73},{25,1},{49,25},{73,49},{2,74}... | collective-permute-start | bytes 2359304 | tf_op jit(solution)/shard_map/ppermute | solution.py:126
  77.5 30.1 %copy-start.16 = (bf16[128,256]{1,0:T(8,128)(2,1)S(1)}, bf16[128,256]{1,0:T(8,128)(2,1)}, u32[]{:S(2)}) copy-start(bf16[128,256]{1,0:T(8,128)(2,1)} %param.11) | copy-start | bytes 196612
  77.5 30.0 %all-to-all-start.1 = ((f32[8,128,128]{2,1,0:T(8,128)}), f32[8,128,128]{2,1,0:T(8,128)S(1)}, u32[]{:S(2)}, u32[]{:S(2)}) async-start(f32[8,128,128]{2,1,0:T(8,128)} %forward_one.1), calls=%async_computation.1 | async-start | bytes 1048576 | tf_op jit(solution)/shard_map/all_to_all | solution.py:121
  95.7 1.2 copy-start.5
  96.9 1.2 copy-start.7
  107.6 3.5 %copy-start.13 = (bf16[128,128]{1,0:T(8,128)(2,1)}, bf16[128,128]{1,0:T(8,128)(2,1)S(1)}, u32[]{:S(2)}) copy-start(bf16[128,128]{1,0:T(8,128)(2,1)S(1)} %reduce_sum.45) | copy-start | bytes 98308
  111.1 14.9 %copy-start.15 = (bf16[128,128]{1,0:T(8,128)(2,1)S(1)}, bf16[128,128]{1,0:T(8,128)(2,1)}, u32[]{:S(2)}) copy-start(bf16[128,128]{1,0:T(8,128)(2,1)} %convolution_convert_fusion.earlier_ref) | copy-start | bytes 98308
  115.3 56.3 %copy-start.6 = (f32[24,128,128]{2,1,0:T(8,128)S(1)}, f32[24,128,128]{2,1,0:T(8,128)}, u32[]{:S(2)}) copy-start(f32[24,128,128]{2,1,0:T(8,128)} %copy-done.5) | copy-start | bytes 4718596
  115.3 55.6 %collective-permute-start.8 = (f16[3088,128]{1,0:T(8,128)(2,1)}, f16[3088,128]{1,0:T(8,128)(2,1)}, u32[]{:S(2)}, u32[]{:S(2)}) collective-permute-start(f16[3088,128]{1,0:T(8,128)(2,1)} %get-tuple-element.18), channel_id=1, source_target_pairs={{0,72},{24,0},{48,24},{72,48},{1,73},{25,1},{49,25},{73,49},{2,74}... | collective-permute-start | bytes 2371592 | tf_op jit(solution)/shard_map/ppermute | solution.py:126
  121.6 49.3 %collective-permute-start.7 = (f16[3088,128]{1,0:T(8,128)(2,1)}, f16[3088,128]{1,0:T(8,128)(2,1)}, u32[]{:S(2)}, u32[]{:S(2)}) collective-permute-start(f16[3088,128]{1,0:T(8,128)(2,1)} %get-tuple-element.17), channel_id=1, source_target_pairs={{0,48},{24,72},{48,0},{72,24},{1,49},{25,73},{49,1},{73,25},{2,50}... | collective-permute-start | bytes 2371592 | tf_op jit(solution)/shard_map/ppermute | solution.py:126
  123.5 47.4 %collective-permute-start.6 = (f16[3088,128]{1,0:T(8,128)(2,1)}, f16[3088,128]{1,0:T(8,128)(2,1)}, u32[]{:S(2)}, u32[]{:S(2)}) collective-permute-start(f16[3088,128]{1,0:T(8,128)(2,1)} %get-tuple-element.16), channel_id=1, source_target_pairs={{0,24},{24,48},{48,72},{72,0},{1,25},{25,49},{49,73},{73,1},{2,26}... | collective-permute-start | bytes 2371592 | tf_op jit(solution)/shard_map/ppermute | solution.py:126
  173.8 9.9 %copy-start.2 = (bf16[24,128,128]{2,1,0:T(8,128)(2,1)S(1)}, bf16[24,128,128]{2,1,0:T(8,128)(2,1)}, u32[]{:S(2)}) copy-start(bf16[24,128,128]{2,1,0:T(8,128)(2,1)} %all-gather.3.refs_1_) | copy-start | bytes 2359300
  175.0 28.2 %all-to-all-start.2 = ((f16[24,144,128]{2,1,0:T(8,128)(2,1)}), f16[24,144,128]{2,1,0:T(8,128)(2,1)}, u32[]{:S(2)}, u32[]{:S(2)}) async-start(f16[24,144,128]{2,1,0:T(8,128)(2,1)} %select_convert_fusion), calls=%async_computation.2 | async-start | bytes 1769472 | tf_op jit(solution)/shard_map/all_to_all | solution.py:121
  183.7 33.0 %collective-permute-start.3 = (bf16[24,128,128]{2,1,0:T(8,128)(2,1)S(1)}, bf16[24,128,128]{2,1,0:T(8,128)(2,1)S(1)}, u32[]{:S(2)}, u32[]{:S(2)}) collective-permute-start(bf16[24,128,128]{2,1,0:T(8,128)(2,1)S(1)} %copy-done.2), channel_id=1, source_target_pairs={{0,24},{24,48},{48,72},{72,0},{1,25},{25,49},{49,73},{73,1},{2,26}... | collective-permute-start | bytes 2359304 | tf_op jit(solution)/shard_map/ppermute | solution.py:126
  185.6 32.0 %collective-permute-start.4 = (bf16[24,128,128]{2,1,0:T(8,128)(2,1)S(1)}, bf16[24,128,128]{2,1,0:T(8,128)(2,1)}, u32[]{:S(2)}, u32[]{:S(2)}) collective-permute-start(bf16[24,128,128]{2,1,0:T(8,128)(2,1)S(1)} %copy-done.2), channel_id=1, source_target_pairs={{0,48},{24,72},{48,0},{72,24},{1,49},{25,73},{49,1},{73,25},{2,50}... | collective-permute-start | bytes 2359304 | tf_op jit(solution)/shard_map/ppermute | solution.py:126
  189.0 37.9 %collective-permute-start.5 = (bf16[24,128,128]{2,1,0:T(8,128)(2,1)S(1)}, bf16[24,128,128]{2,1,0:T(8,128)(2,1)}, u32[]{:S(2)}, u32[]{:S(2)}) collective-permute-start(bf16[24,128,128]{2,1,0:T(8,128)(2,1)S(1)} %copy-done.2), channel_id=1, source_target_pairs={{0,72},{24,0},{48,24},{72,48},{1,73},{25,1},{49,25},{73,49},{2,74}... | collective-permute-start | bytes 2359304 | tf_op jit(solution)/shard_map/ppermute | solution.py:126
  208.1 22.6 %all-to-all-start.3 = ((f32[32,16,128]{2,1,0:T(8,128)}), f32[32,16,128]{2,1,0:T(8,128)S(1)}, u32[]{:S(2)}, u32[]{:S(2)}) async-start(f32[32,16,128]{2,1,0:T(8,128)} %bitcast.50), calls=%async_computation.3 | async-start | bytes 524288 | tf_op jit(solution)/shard_map/all_to_all | solution.py:121
  271.3 20.2 %all-to-all-start.5 = ((f32[32,16,128]{2,1,0:T(8,128)}), f32[32,16,128]{2,1,0:T(8,128)S(1)}, u32[]{:S(2)}, u32[]{:S(2)}) async-start(f32[32,16,128]{2,1,0:T(8,128)} %broadcast_in_dim.58), calls=%async_computation.5 | async-start | bytes 524288 | tf_op jit(solution)/shard_map/all_to_all | solution.py:121
  (6 other events, 6.1 us)
